TPU v7x, 32 devices: a whole 2x2x4 slice. The times are simulated.
32 devices in a mesh: groups: 2 (over y), lat: 4 (over x, core), lon: 4 (over z).
Axes of the slice: x: 2, y: 2, z: 4, core: 2. Of those that a mesh axis runs over, the one named last changes fastest.
Arguments:
- tracers: float32 [256, 256, 128], P(('groups', 'lat'), 'lon'), parts along dimension 0, may hold values from 0.3 to 12.6, as said below
- shifts: float32 [4, 3, 16, 32], P('groups'), parts along dimension 0, may hold values from 0 to 1
- diffusivity: float32 [128], P('lat'), may hold values from 0.02 to 0.2, as said below
- source_patch: int32 [4, 16, 32], P('groups'), parts along dimension 0, may hold values from 0 to 511, as said below
Outputs:
- advanced: float32 [256, 256, 128], P(('groups', 'lat'), 'lon'), parts along dimension 0
There are 2 independent parts, one for each index of `groups`. A program takes and returns all parts, laid end to end along the dimension named above; an argument that names none is the same for every part. Nothing has to cross between parts.
Inputs may be any that keep to these rules, and one draw needn't show every extreme that they name: `source_patch`: entry [s, r, c] is the global index of the departure patch of destination patch (r, c) in step s; the departure patch lies in the same tile of 8 patch columns as the destination, and in the same band of 4 patch rows or in one of the two bands on either side. For each step, tile, destination band and other source band, at most 4 destination patches take their departure patch there, and every destination band has a source band that gives exactly 4. `tracers`: positive mixing ratios. `diffusivity`: positive diffusion numbers.
All inputs are finite; a program needn't handle non-finite values.
Results may differ from a plain program's by a relative error of at most 0.0003.
Values sent between devices are 32-bit elements; how exact they have to be, the bound alone decides.
A program may use at most 64 MiB of HBM per device.

v0:
```python
import math

import jax
import jax.numpy as jnp
from jax import lax
from jax.sharding import PartitionSpec as P

LEV = 4
STEPS = 2
CAP = 4


def from_behind(block, axis, distance):
    devices = range(lax.axis_size(axis))
    route = [(i - distance, i) for i in devices if i - distance in devices]
    return lax.ppermute(block, axis, route)


def extended(cells, sides, width, closed):
    for axis, dim in sides:
        count = lax.axis_size(axis)
        ends = count if closed else count - 1
        head = lax.slice_in_dim(cells, 0, width, axis=dim)
        tail = lax.slice_in_dim(cells, cells.shape[dim] - width, cells.shape[dim], axis=dim)
        cells = jnp.concatenate(
            [
                lax.ppermute(tail, axis, [(i, (i + 1) % count) for i in range(ends)]),
                cells,
                lax.ppermute(head, axis, [((i + 1) % count, i) for i in range(ends)]),
            ],
            axis=dim,
        )
    return cells


def cubic_weights(fraction):
    first_term = -fraction * (fraction - 1.0) * (fraction - 2.0) / 6.0
    second_term = (fraction + 1.0) * (fraction - 1.0) * (fraction - 2.0) / 2.0
    third_term = -(fraction + 1.0) * fraction * (fraction - 2.0) / 2.0
    fourth_term = (fraction + 1.0) * fraction * (fraction - 1.0) / 6.0
    return (first_term, second_term, third_term, fourth_term)


def cubic_matrix(fraction, extent):
    places = jnp.arange(extent)
    running = jnp.zeros(fraction.shape + (extent, extent), jnp.float32)
    for offset, weight in zip(range(-1, 3), cubic_weights(fraction)):
        target_col = jnp.clip(places + offset, 0, extent - 1)
        indicator = (target_col[:, None] == places[None, :]).astype(jnp.float32)
        running = running + weight[..., None, None] * indicator
    return running


def interpolate(patches, fraction_y, fraction_x, fraction_z):
    patch_count = patches.shape[0]
    value_count = patches.shape[2]
    weight_y = cubic_matrix(fraction_y, 8)
    weight_x = cubic_matrix(fraction_x, 8)
    plane_weights = jnp.einsum(
        "nac,nbd->nabcd", weight_y, weight_x, precision=lax.Precision.HIGHEST
    ).reshape(patch_count, 64, 64)
    flat_result = jnp.einsum(
        "nij,njv->niv", plane_weights, patches, precision=lax.Precision.HIGHEST
    )
    stacked = flat_result.reshape(patch_count, 64, LEV, value_count // LEV)
    weight_z = cubic_matrix(fraction_z, LEV)
    levelled = jnp.einsum("nlm,nimt->nilt", weight_z, stacked, precision=lax.Precision.HIGHEST)
    return levelled.reshape(patch_count, 64, value_count)


def to_patches(state_field):
    band_rows = state_field.shape[0] // 8
    band_cols = state_field.shape[1] // 8
    return (
        state_field.reshape(band_rows, 8, band_cols, 8, -1)
        .transpose(0, 2, 1, 3, 4)
        .reshape(band_rows * band_cols, 64, -1)
    )


def from_patches(patches, band_rows, band_cols):
    return (
        patches.reshape(band_rows, band_cols, 8, 8, -1)
        .transpose(0, 2, 1, 3, 4)
        .reshape(band_rows * 8, band_cols * 8, -1)
    )


def column_area(first_row, row_count, total_rows):
    latitude = ((first_row + jnp.arange(row_count)).astype(jnp.float32) + 0.5) * (
        math.pi / total_rows
    ) - 0.5 * math.pi
    return jnp.cos(latitude)


def column_mass(state_field, weights):
    return jnp.sum(weights[:, None, None] * state_field, axis=(0, 1))


def local(tracers, shifts, diffusivity, source_patch):
    lat_count = lax.axis_size("lat")
    lat_index = lax.axis_index("lat")
    lon_index = lax.axis_index("lon")
    row_count, col_count, value_count = tracers.shape
    band_rows = row_count // 8
    band_cols = col_count // 8
    per_device = band_rows * band_cols
    total_cols = source_patch.shape[2]
    band_offsets = (-2, -1, 1, 2)
    weights = column_area(lat_index * row_count, row_count, row_count * lat_count)
    devices = jnp.arange(lat_count)
    slot_range = jnp.arange(CAP)
    state_field = tracers
    target = lax.psum(column_mass(tracers, weights), ("lat", "lon"))
    for step_index in range(STEPS):
        column_ids = lax.dynamic_slice_in_dim(
            source_patch[step_index], lon_index * band_cols, band_cols, 1
        ).reshape(lat_count, per_device)
        fractions = lax.dynamic_slice_in_dim(
            shifts[step_index], lon_index * band_cols, band_cols, 2
        ).reshape(3, lat_count, per_device)
        source_row = column_ids // total_cols
        source_dev = source_row // band_rows
        source_local = (
            source_row % band_rows * band_cols + column_ids % total_cols - lon_index * band_cols
        )
        remote = source_dev != devices[:, None]
        matches = (source_dev[:, :, None] == devices[None, None, :]) & remote[:, :, None]
        slot_ranks = jnp.cumsum(matches.astype(jnp.int32), axis=1) - 1
        slot_of = jnp.sum(jnp.where(matches, slot_ranks, 0), axis=2)
        owned_here = remote & (source_dev == lat_index)
        sending = owned_here[:, :, None] & (slot_of[:, :, None] == slot_range[None, None, :])
        send_local = jnp.sum(jnp.where(sending, source_local[:, :, None], 0), axis=1)
        near_local = jnp.stack(
            [
                lax.dynamic_index_in_dim(send_local, lat_index + offset, 0, keepdims=False)
                for offset in band_offsets
            ]
        )
        own_patches = to_patches(state_field)
        send_patches = own_patches[near_local.reshape(-1)]
        my_dev = lax.dynamic_index_in_dim(source_dev, lat_index, 0, keepdims=False)
        my_slot = lax.dynamic_index_in_dim(slot_of, lat_index, 0, keepdims=False)
        my_local = lax.dynamic_index_in_dim(source_local, lat_index, 0, keepdims=False)
        my_remote = lax.dynamic_index_in_dim(remote, lat_index, 0, keepdims=False)
        my_frac = lax.dynamic_index_in_dim(fractions, lat_index, 1, keepdims=False)
        my_offset = lat_index - my_dev
        pick_index = jnp.where(my_offset < 0, my_offset + 2, my_offset + 1) * CAP + my_slot
        send_frac = jnp.sum(jnp.where(sending[None], fractions[:, :, :, None], 0.0), axis=2)
        near_frac = jnp.stack(
            [
                lax.dynamic_index_in_dim(send_frac, lat_index + offset, 1, keepdims=False)
                for offset in band_offsets
            ],
            axis=1,
        ).reshape(3, -1)
        outgoing = interpolate(send_patches, near_frac[0], near_frac[1], near_frac[2])
        outgoing = outgoing.reshape(4, CAP, 64, value_count)
        arrived = jnp.stack(
            [
                from_behind(outgoing[slot_place], "lat", offset)
                for slot_place, offset in enumerate(band_offsets)
            ]
        )
        arrived = arrived.reshape(4 * CAP, 64, value_count)
        local_done = interpolate(own_patches[my_local], my_frac[0], my_frac[1], my_frac[2])
        finished = jnp.where(my_remote[:, None, None], arrived[pick_index], local_done)
        advected = from_patches(finished, band_rows, band_cols)
        lon_wide = extended(advected, (("lon", 1),), 1, True)
        lat_wide = extended(advected, (("lat", 0),), 1, False)
        laplace = lat_wide[2:] + lat_wide[:-2] + lon_wide[:, 2:] + lon_wide[:, :-2] - 4.0 * advected
        diffused = advected + diffusivity[:, None, None] * laplace
        step_total = lax.psum(column_mass(diffused, weights), ("lat", "lon"))
        state_field = diffused * (target / step_total)[None, None, :]
    return state_field


def solution(mesh):
    return jax.shard_map(
        local,
        mesh=mesh,
        in_specs=(
            P(("groups", "lat"), "lon", None),
            P("groups", None, None, None),
            P("lat"),
            P("groups", None, None),
        ),
        out_specs=P(("groups", "lat"), "lon", None),
        check_vma=False,
    )
```

profile of v0, /device:TPU:0, one launch (start us, length us, event | category | flops | bytes accessed | tf_op | source)
XLA Modules:
  0.0 196.2 jit_solution(16985384277161938453)
XLA Ops:
  9.6 2.9 %fusion.150 = f32[16,64,128]{1,2,0:T(8,128)S(1)} fusion(f32[16,64,64]{2,1,0:T(8,128)} %copy.62, f32[16,64,128]{2,1,0:T(8,128)S(1)} %gather_fusion), kind=kOutput, calls=%fused_computation.360 | convolution fusion | flops 100663296 | bytes 1310720 | tf_op jit(solution)/shard_map/nij,njv->niv/dot_general | solution.py:62
  12.5 2.5 %convolution_bitcast_fusion.1 = f32[16,64,4,32]{1,2,3,0:T(4,128)S(1)} fusion(f32[16,64,4,32]{1,3,2,0:T(8,128)S(1)} %bitcast.153, f32[4,4]{1,0:T(4,128)S(1)} %fusion.111, f32[16]{0:T(128)S(1)} %get-tuple-element.115, f32[4,4]{1,0:T(4,128)S(1)} %fusion.110, f32[16]{0:T(128)S(1)} %get-tuple-element.116, f32[4,4]{1,0:T(4,128)S(1)} %fusion.109, ...), kind=kOutput, calls=%fused_computation.13 | convolution fusion | flops 6293248 | bytes 1049088 | tf_op jit(solution)/shard_map/nlm,nimt->nilt/dot_general | solution.py:67
  19.2 3.7 %collective-permute-start.2 = (f32[4,64,128]{1,2,0:T(8,128)}, f32[4,64,128]{1,2,0:T(8,128)}, u32[]{:S(2)}, u32[]{:S(2)}) collective-permute-start(f32[4,64,128]{1,2,0:T(8,128)} %bitcast.16), channel_id=1, source_target_pairs={{0,4},{4,8},{8,12},{1,5},{5,9},{9,13},{2,6},{6,10},{10,14},{3,7},{... | collective-permute-start | bytes 393224 | tf_op jit(solution)/shard_map/ppermute | solution.py:16
  23.7 6.3 %collective-permute-start.3 = (f32[4,64,128]{1,2,0:T(8,128)}, f32[4,64,128]{1,2,0:T(8,128)}, u32[]{:S(2)}, u32[]{:S(2)}) collective-permute-start(f32[4,64,128]{1,2,0:T(8,128)} %bitcast.18), channel_id=1, source_target_pairs={{0,8},{4,12},{1,9},{5,13},{2,10},{6,14},{3,11},{7,15},{16,24},{20,... | collective-permute-start | bytes 393224 | tf_op jit(solution)/shard_map/ppermute | solution.py:16
  41.7 3.5 %fusion.151 = f32[32,64,128]{1,2,0:T(8,128)S(1)} fusion(f32[32,64,64]{2,1,0:T(8,128)S(1)} %copy-done.1, f32[32,64,128]{2,1,0:T(8,128)S(1)} %gather_fusion.2), kind=kOutput, calls=%fused_computation.361 | convolution fusion | flops 201326592 | bytes 2621440 | tf_op jit(solution)/shard_map/nij,njv->niv/dot_general | solution.py:62
  47.1 5.6 %fusion.4 = f32[32,64,4,32]{1,2,3,0:T(4,128)} fusion(f32[32,64,4,32]{1,3,2,0:T(8,128)S(1)} %bitcast.143, f32[4,4]{1,0:T(4,128)S(1)} %copy-done.10, f32[32]{0:T(128)S(1)} %get-tuple-element.105, f32[4,4]{1,0:T(4,128)S(1)} %copy-done.8, f32[32]{0:T(128)S(1)} %get-tuple-element.106, f32[4,4]{1,0:T(4,128)S(1)} %copy-done.6, f32[32]{0:T(128)S(1)} %get-tuple-element.104, ...), kind=kOutput, calls=%fused_computation.10 | convolution fusion | flops 12586496 | bytes 2097920 | tf_op jit(solution)/shard_map/nlm,nimt->nilt/dot_general | solution.py:67
  53.4 4.8 %copy.73 = f32[32,64,4,32]{3,2,1,0:T(4,128)} copy(f32[32,64,4,32]{1,2,3,0:T(4,128)} %fusion.4) | data formatting | bytes 2097152 | tf_op jit(solution)/shard_map/nlm,nimt->nilt/transpose | solution.py:67
  58.2 4.5 %reshape.1437 = f32[4,8,8,8,128]{4,3,2,1,0:T(8,128)} reshape(f32[32,64,4,32]{3,2,1,0:T(4,128)} %copy.73) | data formatting | bytes 2097152 | tf_op jit(solution)/shard_map/reshape | solution.py:68
  62.9 2.3 %pad_maximum_fusion.8 = f32[4,4,64,128]{2,3,1,0:T(8,128)} fusion(f32[1,4,64,128]{2,3,1,0:T(8,128)} %bitcast.19, f32[1,4,64,128]{2,3,1,0:T(8,128)} %bitcast.17, f32[1,4,64,128]{2,3,1,0:T(8,128)} %bitcast.15, f32[1,4,64,128]{2,3,1,0:T(8,128)} %bitcast.13), kind=kLoop, calls=%fused_computation.34 | loop fusion | flops 393216 | bytes 1048576 | tf_op jit(solution)/shard_map/stack | solution.py:159
  71.5 3.0 %collective-permute-start.5 = (f32[1,64,128]{2,1,0:T(8,128)S(1)}, f32[1,64,128]{2,1,0:T(8,128)S(1)}, u32[]{:S(2)}, u32[]{:S(2)}) collective-permute-start(f32[1,64,128]{2,1,0:T(8,128)S(1)} %get-tuple-element.36), channel_id=1, source_target_pairs={{0,4},{4,8},{8,12},{1,5},{5,9},{9,13},{2,6},{6,10},{10,14},{3,7},{... | collective-permute-start | bytes 98312 | tf_op jit(solution)/shard_map/ppermute | solution.py:27
  74.5 4.8 %collective-permute-start.6 = (f32[32,1,128]{2,1,0:T(1,128)S(1)}, f32[32,1,128]{2,1,0:T(1,128)S(1)}, u32[]{:S(2)}, u32[]{:S(2)}) collective-permute-start(f32[32,1,128]{2,1,0:T(1,128)S(1)} %get-tuple-element.37), channel_id=1, source_target_pairs={{1,0},{2,1},{3,2},{0,3},{5,4},{6,5},{7,6},{4,7},{9,8},{10,9},{11,1... | collective-permute-start | bytes 49160 | tf_op jit(solution)/shard_map/ppermute | solution.py:29
  79.4 3.3 %copy.84 = f32[32,64,64]{2,1,0:T(8,128)} copy(f32[32,64,64]{0,2,1:T(8,128)} %bitcast.142) | data formatting | bytes 1048576 | tf_op jit(solution)/shard_map/reshape | solution.py:61
  84.9 1.9 multiply_reduce_fusion.1
  86.8 30.4 %all-reduce = (f32[128]{0:T(128)S(1)}, f32[128]{0:T(128)S(1)}) all-reduce(f32[128]{0:T(128)S(1)} %get-tuple-element.6, f32[128]{0:T(128)S(1)} %get-tuple-element.5), channel_id=1, replica_groups=mesh['groups'=2,'lat'=4,'lon'=4] {'lat','lon'}, use_global_device_ids=true, to_apply=%region_8.9 | all-reduce | flops 256 | bytes 2048 | tf_op jit(solution)/shard_map/psum | solution.py:114
  121.3 2.5 %convolution_bitcast_fusion = f32[16,64,4,32]{1,2,3,0:T(4,128)S(1)} fusion(f32[16,64,4,32]{1,3,2,0:T(8,128)S(1)} %bitcast.154, f32[16]{0:T(128)S(1)} %copy-done.24, f32[16]{0:T(128)S(1)} %copy-done.25, f32[16]{0:T(128)S(1)} %copy-done.23, f32[16]{0:T(128)S(1)} %copy-done.22, f32[4,4]{1,0:T(4,128)S(1)} %copy-done.10, f32[4,4]{1,0:T(4,128)S(1)} %copy-done.8, ...), kind=kOutput, calls=%fused_computation.12 | convolution fusion | flops 6293248 | bytes 1049088 | tf_op jit(solution)/shard_map/nlm,nimt->nilt/dot_general | solution.py:67
  126.7 3.7 %collective-permute-start.10 = (f32[4,64,128]{1,2,0:T(8,128)S(1)}, f32[4,64,128]{1,2,0:T(8,128)}, u32[]{:S(2)}, u32[]{:S(2)}) collective-permute-start(f32[4,64,128]{1,2,0:T(8,128)S(1)} %bitcast.161), channel_id=1, source_target_pairs={{0,4},{4,8},{8,12},{1,5},{5,9},{9,13},{2,6},{6,10},{10,14},{3,7},{... | collective-permute-start | bytes 393224 | tf_op jit(solution)/shard_map/ppermute | solution.py:16
  130.5 6.3 %collective-permute-start.11 = (f32[4,64,128]{1,2,0:T(8,128)S(1)}, f32[4,64,128]{1,2,0:T(8,128)}, u32[]{:S(2)}, u32[]{:S(2)}) collective-permute-start(f32[4,64,128]{1,2,0:T(8,128)S(1)} %bitcast.162), channel_id=1, source_target_pairs={{0,8},{4,12},{1,9},{5,13},{2,10},{6,14},{3,11},{7,15},{16,24},{20,... | collective-permute-start | bytes 393224 | tf_op jit(solution)/shard_map/ppermute | solution.py:16
  136.8 3.5 %fusion.153 = f32[32,64,128]{1,2,0:T(8,128)S(1)} fusion(f32[32,64,64]{2,1,0:T(8,128)S(1)} %copy-done, f32[32,64,128]{2,1,0:T(8,128)S(1)} %gather_fusion.5), kind=kOutput, calls=%fused_computation.363 | convolution fusion | flops 201326592 | bytes 2621440 | tf_op jit(solution)/shard_map/nij,njv->niv/dot_general | solution.py:62
  140.3 4.5 %fusion.7 = f32[32,64,4,32]{1,2,3,0:T(4,128)S(1)} fusion(f32[32,64,4,32]{1,3,2,0:T(8,128)S(1)} %bitcast.144, f32[32]{0:T(128)S(1)} %copy-done.30, f32[32]{0:T(128)S(1)} %copy-done.31, f32[32]{0:T(128)S(1)} %copy-done.29, f32[32]{0:T(128)S(1)} %copy-done.27, f32[4,4]{1,0:T(4,128)S(1)} %copy-done.10, f32[4,4]{1,0:T(4,128)S(1)} %copy-done.8, ...), kind=kOutput, calls=%fused_computation.11 | convolution fusion | flops 12586496 | bytes 2097920 | tf_op jit(solution)/shard_map/nlm,nimt->nilt/dot_general | solution.py:67
  144.8 3.2 %copy.87 = f32[32,64,4,32]{3,2,1,0:T(4,128)} copy(f32[32,64,4,32]{1,2,3,0:T(4,128)S(1)} %fusion.7) | data formatting | bytes 2097152 | tf_op jit(solution)/shard_map/nlm,nimt->nilt/transpose | solution.py:67
  148.0 3.7 %reshape.1446 = f32[4,8,8,8,128]{4,3,2,1,0:T(8,128)S(1)} reshape(f32[32,64,4,32]{3,2,1,0:T(4,128)} %copy.87) | data formatting | bytes 2097152 | tf_op jit(solution)/shard_map/reshape | solution.py:68
  155.5 3.0 %collective-permute-start.13 = (f32[1,64,128]{2,1,0:T(8,128)S(1)}, f32[1,64,128]{2,1,0:T(8,128)S(1)}, u32[]{:S(2)}, u32[]{:S(2)}) collective-permute-start(f32[1,64,128]{2,1,0:T(8,128)S(1)} %get-tuple-element.28), channel_id=1, source_target_pairs={{0,4},{4,8},{8,12},{1,5},{5,9},{9,13},{2,6},{6,10},{10,14},{3,7},{... | collective-permute-start | bytes 98312 | tf_op jit(solution)/shard_map/ppermute | solution.py:27
  158.7 2.0 %collective-permute-start.15 = (f32[32,1,128]{2,1,0:T(1,128)S(1)}, f32[32,1,128]{2,1,0:T(1,128)S(1)}, u32[]{:S(2)}, u32[]{:S(2)}) collective-permute-start(f32[32,1,128]{2,1,0:T(1,128)S(1)} %get-tuple-element.30), channel_id=1, source_target_pairs={{0,1},{1,2},{2,3},{3,0},{4,5},{5,6},{6,7},{7,4},{8,9},{9,10},{10,1... | collective-permute-start | bytes 49160 | tf_op jit(solution)/shard_map/ppermute | solution.py:27
  165.0 29.8 %psum.23 = f32[128]{0:T(128)S(1)} all-reduce(f32[128]{0:T(128)S(1)} %multiply_reduce_fusion), channel_id=1, replica_groups=mesh['groups'=2,'lat'=4,'lon'=4] {'lat','lon'}, use_global_device_ids=true, to_apply=%region_13.14 | all-reduce | flops 128 | bytes 1024 | tf_op jit(solution)/shard_map/psum | solution.py:173
  (220 shorter events, 53.5 us)
Async XLA Ops:
  5.4 27.5 %copy-start.11 = (s32[4,32]{1,0:T(4,128)}, s32[4,32]{1,0:T(4,128)S(1)}, u32[]{:S(2)}) copy-start(s32[4,32]{1,0:T(4,128)S(1)} %select_reduce_fusion.3) | copy-start | bytes 1540
  15.0 17.8 %copy-start.21 = (pred[4,32]{1,0:T(4,128)(4,1)S(1)}, pred[4,32]{1,0:T(4,128)(4,1)}, u32[]{:S(2)}) copy-start(pred[4,32]{1,0:T(4,128)(4,1)} %copy-done.20) | copy-start | bytes 388
  15.2 47.7 %collective-permute-start = (f32[4,64,128]{1,2,0:T(8,128)S(1)}, f32[4,64,128]{1,2,0:T(8,128)}, u32[]{:S(2)}, u32[]{:S(2)}) collective-permute-start(f32[4,64,128]{1,2,0:T(8,128)S(1)} %bitcast.158), channel_id=1, source_target_pairs={{8,0},{12,4},{9,1},{13,5},{10,2},{14,6},{11,3},{15,7},{24,16},{28,... | collective-permute-start | bytes 393224 | tf_op jit(solution)/shard_map/ppermute | solution.py:16
  17.2 45.7 %collective-permute-start.1 = (f32[4,64,128]{1,2,0:T(8,128)}, f32[4,64,128]{1,2,0:T(8,128)}, u32[]{:S(2)}, u32[]{:S(2)}) collective-permute-start(f32[4,64,128]{1,2,0:T(8,128)} %bitcast.14), channel_id=1, source_target_pairs={{4,0},{8,4},{12,8},{5,1},{9,5},{13,9},{6,2},{10,6},{14,10},{7,3},{... | collective-permute-start | bytes 393224 | tf_op jit(solution)/shard_map/ppermute | solution.py:16
  19.2 43.6 %collective-permute-start.2 = (f32[4,64,128]{1,2,0:T(8,128)}, f32[4,64,128]{1,2,0:T(8,128)}, u32[]{:S(2)}, u32[]{:S(2)}) collective-permute-start(f32[4,64,128]{1,2,0:T(8,128)} %bitcast.16), channel_id=1, source_target_pairs={{0,4},{4,8},{8,12},{1,5},{5,9},{9,13},{2,6},{6,10},{10,14},{3,7},{... | collective-permute-start | bytes 393224 | tf_op jit(solution)/shard_map/ppermute | solution.py:16
  23.7 39.2 %collective-permute-start.3 = (f32[4,64,128]{1,2,0:T(8,128)}, f32[4,64,128]{1,2,0:T(8,128)}, u32[]{:S(2)}, u32[]{:S(2)}) collective-permute-start(f32[4,64,128]{1,2,0:T(8,128)} %bitcast.18), channel_id=1, source_target_pairs={{0,8},{4,12},{1,9},{5,13},{2,10},{6,14},{3,11},{7,15},{16,24},{20,... | collective-permute-start | bytes 393224 | tf_op jit(solution)/shard_map/ppermute | solution.py:16
  68.3 11.1 %copy-start.17 = (pred[4,32]{1,0:T(4,128)(4,1)S(1)}, pred[4,32]{1,0:T(4,128)(4,1)}, u32[]{:S(2)}) copy-start(pred[4,32]{1,0:T(4,128)(4,1)} %copy-done.16) | copy-start | bytes 388
  70.2 14.7 %collective-permute-start.4 = (f32[1,64,128]{2,1,0:T(8,128)S(1)}, f32[1,64,128]{2,1,0:T(8,128)S(1)}, u32[]{:S(2)}, u32[]{:S(2)}) collective-permute-start(f32[1,64,128]{2,1,0:T(8,128)S(1)} %get-tuple-element.35), channel_id=1, source_target_pairs={{4,0},{8,4},{12,8},{5,1},{9,5},{13,9},{6,2},{10,6},{14,10},{7,3},{... | collective-permute-start | bytes 98312 | tf_op jit(solution)/shard_map/ppermute | solution.py:29
  71.5 13.4 %collective-permute-start.5 = (f32[1,64,128]{2,1,0:T(8,128)S(1)}, f32[1,64,128]{2,1,0:T(8,128)S(1)}, u32[]{:S(2)}, u32[]{:S(2)}) collective-permute-start(f32[1,64,128]{2,1,0:T(8,128)S(1)} %get-tuple-element.36), channel_id=1, source_target_pairs={{0,4},{4,8},{8,12},{1,5},{5,9},{9,13},{2,6},{6,10},{10,14},{3,7},{... | collective-permute-start | bytes 98312 | tf_op jit(solution)/shard_map/ppermute | solution.py:27
  74.5 9.7 %collective-permute-start.6 = (f32[32,1,128]{2,1,0:T(1,128)S(1)}, f32[32,1,128]{2,1,0:T(1,128)S(1)}, u32[]{:S(2)}, u32[]{:S(2)}) collective-permute-start(f32[32,1,128]{2,1,0:T(1,128)S(1)} %get-tuple-element.37), channel_id=1, source_target_pairs={{1,0},{2,1},{3,2},{0,3},{5,4},{6,5},{7,6},{4,7},{9,8},{10,9},{11,1... | collective-permute-start | bytes 49160 | tf_op jit(solution)/shard_map/ppermute | solution.py:29
  79.3 5.5 %collective-permute-start.7 = (f32[32,1,128]{2,1,0:T(1,128)S(1)}, f32[32,1,128]{2,1,0:T(1,128)S(1)}, u32[]{:S(2)}, u32[]{:S(2)}) collective-permute-start(f32[32,1,128]{2,1,0:T(1,128)S(1)} %get-tuple-element.38), channel_id=1, source_target_pairs={{0,1},{1,2},{2,3},{3,0},{4,5},{5,6},{6,7},{7,4},{8,9},{9,10},{10,1... | collective-permute-start | bytes 49160 | tf_op jit(solution)/shard_map/ppermute | solution.py:27
  123.8 13.0 %copy-start = (f32[32,64,64]{2,1,0:T(8,128)S(1)}, f32[32,64,64]{2,1,0:T(8,128)}, u32[]{:S(2)}) copy-start(f32[32,64,64]{2,1,0:T(8,128)} %copy.84) | copy-start | bytes 1572868
  123.9 27.8 %collective-permute-start.8 = (f32[4,64,128]{1,2,0:T(8,128)S(1)}, f32[4,64,128]{1,2,0:T(8,128)S(1)}, u32[]{:S(2)}, u32[]{:S(2)}) collective-permute-start(f32[4,64,128]{1,2,0:T(8,128)S(1)} %bitcast.159), channel_id=1, source_target_pairs={{8,0},{12,4},{9,1},{13,5},{10,2},{14,6},{11,3},{15,7},{24,16},{28,... | collective-permute-start | bytes 393224 | tf_op jit(solution)/shard_map/ppermute | solution.py:16
  125.4 26.4 %collective-permute-start.9 = (f32[4,64,128]{1,2,0:T(8,128)S(1)}, f32[4,64,128]{1,2,0:T(8,128)}, u32[]{:S(2)}, u32[]{:S(2)}) collective-permute-start(f32[4,64,128]{1,2,0:T(8,128)S(1)} %bitcast.160), channel_id=1, source_target_pairs={{4,0},{8,4},{12,8},{5,1},{9,5},{13,9},{6,2},{10,6},{14,10},{7,3},{... | collective-permute-start | bytes 393224 | tf_op jit(solution)/shard_map/ppermute | solution.py:16
  126.7 25.0 %collective-permute-start.10 = (f32[4,64,128]{1,2,0:T(8,128)S(1)}, f32[4,64,128]{1,2,0:T(8,128)}, u32[]{:S(2)}, u32[]{:S(2)}) collective-permute-start(f32[4,64,128]{1,2,0:T(8,128)S(1)} %bitcast.161), channel_id=1, source_target_pairs={{0,4},{4,8},{8,12},{1,5},{5,9},{9,13},{2,6},{6,10},{10,14},{3,7},{... | collective-permute-start | bytes 393224 | tf_op jit(solution)/shard_map/ppermute | solution.py:16
  130.5 9.8 %copy-start.27 = (f32[32]{0:T(128)S(1)}, f32[32]{0:T(128)}, u32[]{:S(2)}) copy-start(f32[32]{0:T(128)} %get-tuple-element.9) | copy-start | bytes 388
  130.5 9.8 %copy-start.29 = (f32[32]{0:T(128)S(1)}, f32[32]{0:T(128)}, u32[]{:S(2)}) copy-start(f32[32]{0:T(128)} %get-tuple-element.83) | copy-start | bytes 388
  130.5 9.8 %copy-start.30 = (f32[32]{0:T(128)S(1)}, f32[32]{0:T(128)}, u32[]{:S(2)}) copy-start(f32[32]{0:T(128)} %get-tuple-element.84) | copy-start | bytes 388
  130.5 9.8 %copy-start.31 = (f32[32]{0:T(128)S(1)}, f32[32]{0:T(128)}, u32[]{:S(2)}) copy-start(f32[32]{0:T(128)} %get-tuple-element.85) | copy-start | bytes 388
  130.5 21.2 %collective-permute-start.11 = (f32[4,64,128]{1,2,0:T(8,128)S(1)}, f32[4,64,128]{1,2,0:T(8,128)}, u32[]{:S(2)}, u32[]{:S(2)}) collective-permute-start(f32[4,64,128]{1,2,0:T(8,128)S(1)} %bitcast.162), channel_id=1, source_target_pairs={{0,8},{4,12},{1,9},{5,13},{2,10},{6,14},{3,11},{7,15},{16,24},{20,... | collective-permute-start | bytes 393224 | tf_op jit(solution)/shard_map/ppermute | solution.py:16
  154.2 10.0 %collective-permute-start.12 = (f32[1,64,128]{2,1,0:T(8,128)S(1)}, f32[1,64,128]{2,1,0:T(8,128)S(1)}, u32[]{:S(2)}, u32[]{:S(2)}) collective-permute-start(f32[1,64,128]{2,1,0:T(8,128)S(1)} %get-tuple-element.27), channel_id=1, source_target_pairs={{4,0},{8,4},{12,8},{5,1},{9,5},{13,9},{6,2},{10,6},{14,10},{7,3},{... | collective-permute-start | bytes 98312 | tf_op jit(solution)/shard_map/ppermute | solution.py:29
  155.5 8.7 %collective-permute-start.13 = (f32[1,64,128]{2,1,0:T(8,128)S(1)}, f32[1,64,128]{2,1,0:T(8,128)S(1)}, u32[]{:S(2)}, u32[]{:S(2)}) collective-permute-start(f32[1,64,128]{2,1,0:T(8,128)S(1)} %get-tuple-element.28), channel_id=1, source_target_pairs={{0,4},{4,8},{8,12},{1,5},{5,9},{9,13},{2,6},{6,10},{10,14},{3,7},{... | collective-permute-start | bytes 98312 | tf_op jit(solution)/shard_map/ppermute | solution.py:27
  158.6 3.8 %collective-permute-start.14 = (f32[32,1,128]{2,1,0:T(1,128)S(1)}, f32[32,1,128]{2,1,0:T(1,128)S(1)}, u32[]{:S(2)}, u32[]{:S(2)}) collective-permute-start(f32[32,1,128]{2,1,0:T(1,128)S(1)} %get-tuple-element.29), channel_id=1, source_target_pairs={{1,0},{2,1},{3,2},{0,3},{5,4},{6,5},{7,6},{4,7},{9,8},{10,9},{11,1... | collective-permute-start | bytes 49160 | tf_op jit(solution)/shard_map/ppermute | solution.py:29
  158.7 5.6 %collective-permute-start.15 = (f32[32,1,128]{2,1,0:T(1,128)S(1)}, f32[32,1,128]{2,1,0:T(1,128)S(1)}, u32[]{:S(2)}, u32[]{:S(2)}) collective-permute-start(f32[32,1,128]{2,1,0:T(1,128)S(1)} %get-tuple-element.30), channel_id=1, source_target_pairs={{0,1},{1,2},{2,3},{3,0},{4,5},{5,6},{6,7},{7,4},{8,9},{9,10},{10,1... | collective-permute-start | bytes 49160 | tf_op jit(solution)/shard_map/ppermute | solution.py:27
  (24 other events, 95.2 us)
where the time goes:
time: 197 us; the launch traced here: 196 us
  blocking collectives  60.2 us (31%)
  starting transfers between devices  40.9 us (21%)
  local copies, waits for them, and re-layouts  39.2 us (20%)
  matrix products  26.7 us (14%)
  other arithmetic  24.1 us (12%)
  waiting for transfers between devices  4.2 us (2%)
    psum x1, blocking collectives, local(): target = lax.psum(column_mass(tracers, weights), ('lat', 'lon'))  30.4 us
    psum x1, blocking collectives, local(): step_total = lax.psum(column_mass(diffused, weights), ('lat', 'lon'))  29.8 us
    ppermute x8, starting transfers between devices, from_behind(): return lax.ppermute(block, axis, route)  25.3 us
    dot_general x4, matrix products, interpolate(): jnp.einsum('nlm,nimt->nilt', weight_z, stacked, precision=lax.Precision.H...  15.1 us
    dot_general x4, matrix products, interpolate(): jnp.einsum('nij,njv->niv', plane_weights, patches, precision=lax.Precisio...  11.6 us
    reshape x2, local copies, waits for them, and re-layouts, interpolate(): return levelled.reshape(patch_count, 64, value_count)  8.25 us
    ppermute x4, starting transfers between devices, extended(): lax.ppermute(tail, axis, [(i, (i + 1) % count) for i in range(ends)])  8.08 us
    transpose x2, local copies, waits for them, and re-layouts, interpolate(): jnp.einsum('nlm,nimt->nilt', weight_z, stacked, precision=lax.Precision.H...  8.02 us
  transfers between devices with their start and end apart: 16, of which 3 were waited for; matrix products, arithmetic and copies ran while one was open for 28% of the time, Pallas kernels for 0%

commit v1 on v0

v1 whole, which is shorter than its diff:
```python
import functools
import math

import jax
import jax.numpy as jnp
from jax import lax
from jax.experimental import pallas as pl
from jax.experimental.pallas import tpu as pltpu
from jax.sharding import PartitionSpec as P

LEV = 4
STEPS = 2
CAP = 4
OFFSETS = (-2, -1, 1, 2)
SENT_FIRST = (0, 3, 1, 2)
MESH = pl.DeviceIdType.MESH


def column_area(first_row, row_count, total_rows):
    latitude = ((first_row + jnp.arange(row_count)).astype(jnp.float32) + 0.5) * (
        math.pi / total_rows
    ) - 0.5 * math.pi
    return jnp.cos(latitude)


def cubic_weights(s):
    return (
        -s * (s - 1.0) * (s - 2.0) * (1.0 / 6.0),
        (s + 1.0) * (s - 1.0) * (s - 2.0) * 0.5,
        -(s + 1.0) * s * (s - 2.0) * 0.5,
        (s + 1.0) * s * (s - 1.0) * (1.0 / 6.0),
    )


def place_weights(w, place, last):
    a, b, c, d = w
    return (
        jnp.where(place == 0, 0.0, a),
        b + jnp.where(place == 0, a, 0.0) + jnp.where(place == last, c + d, 0.0),
        jnp.where(place == last, 0.0, c + jnp.where(place == last - 1, d, 0.0)),
        jnp.where(place >= last - 1, 0.0, d),
    )


def interpolate(rows, fractions, ratio):
    values = rows[0].shape[1]
    step = values // LEV
    column = lax.broadcasted_iota(jnp.int32, (8, values), 0)
    level = lax.broadcasted_iota(jnp.int32, (8, values), 1) // step
    sy, sx, sz = (jnp.full((8, values), s, jnp.float32) for s in fractions)
    a, b, c, d = cubic_weights(sy)
    ab, cd = a + b, c + d
    bcd = b + cd
    x = rows
    if ratio is not None:
        x = [r * ratio for r in x]
    out = [ab * x[0] + c * x[1] + d * x[2]]
    for i in range(1, 6):
        out.append(a * x[i - 1] + b * x[i] + c * x[i + 1] + d * x[i + 2])
    out.append(a * x[5] + b * x[6] + cd * x[7])
    out.append(a * x[6] + bcd * x[7])
    wx = place_weights(cubic_weights(sx), column, 7)
    wz = place_weights(cubic_weights(sz), level, LEV - 1)
    done = []
    for v in out:
        v = (
            wx[0] * pltpu.roll(v, 1, 0)
            + wx[1] * v
            + wx[2] * pltpu.roll(v, 7, 0)
            + wx[3] * pltpu.roll(v, 6, 0)
        )
        v = (
            wz[0] * pltpu.roll(v, step, 1)
            + wz[1] * v
            + wz[2] * pltpu.roll(v, values - step, 1)
            + wz[3] * pltpu.roll(v, values - 2 * step, 1)
        )
        done.append(v)
    return done


def kernel(
    br, bc, lats, lons,
    ti, tf, tr, out,
    st, arr, ia, snd, adv, outbuf, side_out, side_in, ka_out, ka_in, mass_out, mass_in,
    load_sem, store_sem, psend, precv, hsend, hrecv, ksend, krecv, msend, mrecv,
):
    np_ = br * bc
    rows = br * 8
    peers = lats * lons
    values = tr.shape[-1]
    lat = lax.axis_index("lat")
    lon = lax.axis_index("lon")
    kappa0 = STEPS * 3 * np_
    area0 = kappa0 + rows
    w0 = area0 + rows
    send0, arrive0, local0, pick0 = 0, 4 * CAP, 8 * CAP, 8 * CAP + np_
    per_step = 8 * CAP + 2 * np_

    loads = [
        pltpu.make_async_copy(
            tr.at[:, :, c], st.at[0, pl.ds(c * br, br)], load_sem.at[c]
        )
        for c in range(bc)
    ]
    for copy in loads:
        copy.start()

    zero = jnp.zeros((8, values), jnp.float32)
    for s in range(STEPS):
        for c in range(bc):
            adv[s, c, 0] = zero
            adv[s, c, rows + 1] = zero
    ka_in[...] = jnp.zeros_like(ka_in)
    ka_out[0] = jnp.full((1, values), tf[kappa0] * tf[area0], jnp.float32)
    ka_out[1] = jnp.full(
        (1, values), tf[kappa0 + rows - 1] * tf[area0 + rows - 1], jnp.float32
    )

    def peer(k):
        return {
            "lat": lax.rem(lat + k // lons, lats),
            "lon": lax.rem(lon + lax.rem(k, lons), lons),
        }

    barrier = pltpu.get_barrier_semaphore()

    def greet(k, _):
        pl.semaphore_signal(barrier, inc=1, device_id=peer(k), device_id_type=MESH)
        return 0

    lax.fori_loop(1, peers, greet, 0)
    pl.semaphore_wait(barrier, peers - 1)

    def in_range(offset):
        return (lat + offset >= 0) & (lat + offset < lats)

    def patch_copy(s, o):
        return pltpu.make_async_remote_copy(
            src_ref=snd.at[s, o],
            dst_ref=arr.at[s, 3 - o],
            send_sem=psend.at[s, o],
            recv_sem=precv.at[s, 3 - o],
            device_id={"lat": jnp.clip(lat + OFFSETS[o], 0, lats - 1), "lon": lon},
            device_id_type=MESH,
        )

    def ka_copy(i):
        return pltpu.make_async_remote_copy(
            src_ref=ka_out.at[i],
            dst_ref=ka_in.at[1 - i],
            send_sem=ksend.at[i],
            recv_sem=krecv.at[1 - i],
            device_id={"lat": jnp.clip(lat + 2 * i - 1, 0, lats - 1), "lon": lon},
            device_id_type=MESH,
        )

    def row_copy(s, i):
        return pltpu.make_async_remote_copy(
            src_ref=adv.at[s, :, rows if i else 1],
            dst_ref=adv.at[s, :, 0 if i else rows + 1],
            send_sem=hsend.at[s, i],
            recv_sem=hrecv.at[s, 1 - i],
            device_id={"lat": jnp.clip(lat + 2 * i - 1, 0, lats - 1), "lon": lon},
            device_id_type=MESH,
        )

    def column_copy(s, i):
        return pltpu.make_async_remote_copy(
            src_ref=side_out.at[s, i],
            dst_ref=side_in.at[s, 1 - i],
            send_sem=hsend.at[s, 2 + i],
            recv_sem=hrecv.at[s, 3 - i],
            device_id={"lat": lat, "lon": lax.rem(lon + lons + 2 * i - 1, lons)},
            device_id_type=MESH,
        )

    def send_patches(s):
        for o in SENT_FIRST:
            for j in range(CAP):
                snd[s, o, j] = st[s, ti[s * per_step + send0 + o * CAP + j]]

            @pl.when(in_range(OFFSETS[o]))
            def _():
                patch_copy(s, o).start()

    def fractions(s, e):
        return tuple(tf[(s * 3 + i) * np_ + e] for i in range(3))

    def masses(s):
        def send(k, _):
            pltpu.make_async_remote_copy(
                src_ref=mass_out.at[s],
                dst_ref=mass_in.at[s, k],
                send_sem=msend.at[s],
                recv_sem=mrecv.at[s],
                device_id=peer(k),
                device_id_type=MESH,
            ).start()
            return 0

        lax.fori_loop(1, peers, send, 0)

    def masses_sum(s):
        others = mass_in.at[s, pl.ds(1, peers - 1)]
        pltpu.make_async_copy(others, others, mrecv.at[s]).wait()
        return jnp.sum(mass_in[s], axis=0)

    def advect(s, ratio):
        def own(q, _):
            c, r = q // br, lax.rem(q, br)
            e = r * bc + c
            block = st[s, ti[s * per_step + local0 + e]]
            done = interpolate([block[i] for i in range(8)], fractions(s, e), ratio)
            for i in range(8):
                adv[s, c, 1 + r * 8 + i] = done[i]
            return 0

        lax.fori_loop(0, np_, own, 0)
        for o in (1, 2, 0, 3):

            @pl.when(in_range(OFFSETS[o]))
            def _():
                patch_copy(s, 3 - o).wait_recv()

                def come(j, _):
                    e = ti[s * per_step + arrive0 + o * CAP + j]
                    block = arr[s, o, j]
                    done = interpolate(
                        [block[i] for i in range(8)], fractions(s, e), ratio
                    )
                    for i in range(8):
                        ia[s, o * CAP + j, i] = done[i]
                    return 0

                lax.fori_loop(0, CAP, come, 0)

        def join(q, total):
            c, r = q // br, lax.rem(q, br)
            e = r * bc + c
            pick = ti[s * per_step + pick0 + e]
            block = ia[s, jnp.maximum(pick, 0)]
            far = jnp.full((8, values), pick, jnp.int32) >= 0
            for i in range(8):
                v = jnp.where(far, block[i], adv[s, c, 1 + r * 8 + i])
                adv[s, c, 1 + r * 8 + i] = v
                total = total + tf[w0 + r * 8 + i] * v
            return total

        total = lax.fori_loop(0, np_, join, zero)
        for i in range(2):

            @pl.when(in_range(2 * i - 1))
            def _():
                row_copy(s, i).start()

        for i in range(rows):
            side_out[s, 0, i : i + 1] = adv[s, 0, 1 + i][0:1]
            side_out[s, 1, i : i + 1] = adv[s, bc - 1, 1 + i][7:8]
        for i in range(2):
            column_copy(s, i).start()
        first = functools.reduce(jnp.add, [adv[s, c, 1] for c in range(bc)])
        last = functools.reduce(jnp.add, [adv[s, c, rows] for c in range(bc)])
        return total + first * ka_in[0] + last * ka_in[1]

    def wait_halos(s):
        for i in range(2):

            @pl.when(in_range(2 * i - 1))
            def _():
                row_copy(s, 1 - i).wait_recv()

            column_copy(s, 1 - i).wait_recv()

    column = lax.broadcasted_iota(jnp.int32, (8, values), 0)

    def diffused_row(s, row):
        here = [adv[s, c, 1 + row] for c in range(bc)]
        ahead = [pltpu.roll(v, 7, 0) for v in here]
        behind = [pltpu.roll(v, 1, 0) for v in here]
        west = jnp.broadcast_to(side_in[s, 0, pl.ds(row, 1)], (8, values))
        east = jnp.broadcast_to(side_in[s, 1, pl.ds(row, 1)], (8, values))
        kappa = tf[kappa0 + row]
        result = []
        for c in range(bc):
            e = jnp.where(column == 7, east if c == bc - 1 else ahead[c + 1], ahead[c])
            w = jnp.where(column == 0, west if c == 0 else behind[c - 1], behind[c])
            lap = adv[s, c, row] + adv[s, c, row + 2] + e + w - 4.0 * here[c]
            result.append(here[c] + kappa * lap)
        return result

    for i in range(2):

        @pl.when(in_range(2 * i - 1))
        def _():
            ka_copy(i).start()

    for copy in loads:
        copy.wait()

    send_patches(0)

    def target_row(row, total):
        parts = [st[0, c * br + row // 8, lax.rem(row, 8)] for c in range(bc)]
        return total + tf[area0 + row] * functools.reduce(jnp.add, parts)

    target_part = lax.fori_loop(0, rows, target_row, zero)
    for i in range(2):

        @pl.when(in_range(2 * i - 1))
        def _():
            ka_copy(1 - i).wait_recv()

    total = advect(0, None)
    both = jnp.concatenate(
        [
            jnp.sum(total, axis=0, keepdims=True),
            jnp.sum(target_part, axis=0, keepdims=True),
        ],
        axis=0,
    )
    mass_out[0] = both
    mass_in[0, 0] = both
    masses(0)
    wait_halos(0)

    def first_step(row, _):
        done = diffused_row(0, row)
        for c in range(bc):
            st[1, c * br + row // 8, lax.rem(row, 8)] = done[c]
        return 0

    lax.fori_loop(0, rows, first_step, 0)
    send_patches(1)
    sums = masses_sum(0)
    target = sums[1:2]
    ratio = jnp.broadcast_to(target / sums[0:1], (8, values))
    total = advect(1, ratio)
    both = jnp.broadcast_to(jnp.sum(total, axis=0, keepdims=True), (2, values))
    mass_out[1] = both
    mass_in[1, 0] = both
    masses(1)
    wait_halos(1)
    ratio = jnp.broadcast_to(target / masses_sum(1)[0:1], (8, values))

    stores = []
    for r in range(br):

        def last_step(i, _):
            done = diffused_row(1, r * 8 + i)
            for c in range(bc):
                outbuf[r, i, c] = done[c] * ratio
            return 0

        lax.fori_loop(0, 8, last_step, 0)
        copy = pltpu.make_async_copy(outbuf.at[r], out.at[r], store_sem.at[r])
        copy.start()
        stores.append(copy)

    for s in range(STEPS):
        for o in range(4):

            @pl.when(in_range(OFFSETS[o]))
            def _():
                patch_copy(s, o).wait_send()

        for i in range(2):

            @pl.when(in_range(2 * i - 1))
            def _():
                row_copy(s, i).wait_send()

            column_copy(s, i).wait_send()
        others = mass_in.at[s, pl.ds(1, peers - 1)]
        pltpu.make_async_copy(others, others, msend.at[s]).wait()
    for i in range(2):

        @pl.when(in_range(2 * i - 1))
        def _():
            ka_copy(i).wait_send()

    for copy in stores:
        copy.wait()


def tables(source_patch, shifts, diffusivity, br, bc, rows):
    lats = lax.axis_size("lat")
    lat = lax.axis_index("lat")
    lon = lax.axis_index("lon")
    np_ = br * bc
    total_cols = source_patch.shape[2]
    padded = jnp.pad(
        source_patch, ((0, 0), (2 * br, 2 * br), (0, 0)), constant_values=-1
    )
    near = lax.dynamic_slice(
        padded, (0, lat * br, lon * bc), (STEPS, 5 * br, bc)
    ).reshape(STEPS, 5, np_)
    source_row = near // total_cols
    source_dev = source_row // br
    source_q = (near % total_cols - lon * bc) * br + source_row % br
    entries = jnp.arange(np_)
    earlier = entries[None, :] < entries[:, None]
    same = source_dev[..., :, None] == source_dev[..., None, :]
    rank = jnp.sum((same & earlier).astype(jnp.int32), axis=-1)
    outer = jnp.array([0, 1, 3, 4])
    relative = source_dev[:, 2] - lat
    slots = jnp.arange(CAP)
    from_here = source_dev[:, outer] == lat
    chosen = from_here[..., None] & (rank[:, outer][..., None] == slots)
    send = jnp.sum(jnp.where(chosen, source_q[:, outer][..., None], 0), axis=2)
    arrives = relative[:, None, :] == jnp.array(OFFSETS)[None, :, None]
    chosen = arrives[..., None] & (rank[:, 2][:, None, :, None] == slots)
    arrive = jnp.sum(jnp.where(chosen, entries[None, None, :, None], 0), axis=2)
    is_local = relative == 0
    local = jnp.where(is_local, source_q[:, 2], 0)
    place = jnp.where(relative < 0, relative + 2, relative + 1) * CAP + rank[:, 2]
    pick = jnp.where(is_local, -1, place)
    ti = jnp.concatenate(
        [send.reshape(STEPS, -1), arrive.reshape(STEPS, -1), local, pick], axis=1
    ).reshape(-1)
    mine = lax.dynamic_slice(
        shifts, (0, 0, lat * br, lon * bc), (STEPS, 3, br, bc)
    ).reshape(-1)
    area = column_area(lat * rows, rows, rows * lats)
    ka = diffusivity * area
    w0 = area - 2.0 * ka + jnp.pad(ka[1:], (0, 1)) + jnp.pad(ka[:-1], (1, 0))
    tf = jnp.concatenate([mine, diffusivity, area, w0])
    return ti.astype(jnp.int32), tf


def local(lats, lons, tracers, shifts, diffusivity, source_patch):
    rows, cols, values = tracers.shape
    br, bc = rows // 8, cols // 8
    np_ = br * bc
    ti, tf = tables(source_patch, shifts, diffusivity, br, bc, rows)
    tile = (8, 8, values)
    peers = lats * lons
    dma = pltpu.SemaphoreType.DMA
    f32 = jnp.float32
    result = pl.pallas_call(
        functools.partial(kernel, br, bc, lats, lons),
        out_shape=jax.ShapeDtypeStruct((br, 8, bc, 8, values), f32),
        in_specs=[
            pl.BlockSpec(memory_space=pltpu.SMEM),
            pl.BlockSpec(memory_space=pltpu.SMEM),
            pl.BlockSpec(memory_space=pl.ANY),
        ],
        out_specs=pl.BlockSpec(memory_space=pl.ANY),
        scratch_shapes=[
            pltpu.VMEM((STEPS, np_) + tile, f32),
            pltpu.VMEM((STEPS, 4, CAP) + tile, f32),
            pltpu.VMEM((STEPS, 4 * CAP) + tile, f32),
            pltpu.VMEM((STEPS, 4, CAP) + tile, f32),
            pltpu.VMEM((STEPS, bc, rows + 2, 8, values), f32),
            pltpu.VMEM((br, 8, bc, 8, values), f32),
            pltpu.VMEM((STEPS, 2, rows, values), f32),
            pltpu.VMEM((STEPS, 2, rows, values), f32),
            pltpu.VMEM((2, 1, values), f32),
            pltpu.VMEM((2, 1, values), f32),
            pltpu.VMEM((STEPS, 2, values), f32),
            pltpu.VMEM((STEPS, peers, 2, values), f32),
            dma((bc,)),
            dma((br,)),
            dma((STEPS, 4)),
            dma((STEPS, 4)),
            dma((STEPS, 4)),
            dma((STEPS, 4)),
            dma((2,)),
            dma((2,)),
            dma((STEPS,)),
            dma((STEPS,)),
        ],
        compiler_params=pltpu.CompilerParams(
            collective_id=0, has_side_effects=True, vmem_limit_bytes=32 * 1024 * 1024
        ),
    )(ti, tf, tracers.reshape(br, 8, bc, 8, values))
    return result.reshape(rows, cols, values)


def solution(mesh):
    return jax.shard_map(
        functools.partial(local, mesh.shape["lat"], mesh.shape["lon"]),
        mesh=mesh,
        in_specs=(
            P(("groups", "lat"), "lon", None),
            P("groups", None, None, None),
            P("lat"),
            P("groups", None, None),
        ),
        out_specs=P(("groups", "lat"), "lon", None),
        check_vma=False,
    )
```

time: 197 us -> 40.5 us (0.21)
  blocking collectives: 60.2 us -> 0 us
  starting transfers between devices: 40.9 us -> 0 us
  local copies, waits for them, and re-layouts: 39.2 us -> 7.03 us
  Pallas kernels: 0 us -> 31.9 us
  matrix products: 26.7 us -> 0 us
  other arithmetic: 24.1 us -> 1.23 us
  waiting for transfers between devices: 4.2 us -> 0 us
    psum x2 -> x0, blocking collectives: 60.2 us -> none  [the longest x1 30.4 us: local(): target = lax.psum(column_mass(tracers, weights), ('lat', 'lon'))]
    ppermute x16 -> x0, starting transfers between devices: 40.9 us -> none  [the longest x8 25.3 us: from_behind(): return lax.ppermute(block, axis, route)]
    pallas_call x0 -> x1, Pallas kernels: none -> 31.9 us  [local(): pl.pallas_call(functools.partial(kernel, br, bc, lats, lons), out_shape=j...]
    dot_general x8 -> x0, matrix products: 26.7 us -> none  [the longest x4 15.1 us: interpolate(): jnp.einsum('nlm,nimt->nilt', weight_z, stacked, precision=lax.Precision.H...]
    reshape x10 -> x5, local copies, waits for them, and re-layouts: 16.5 us -> 0.43 us  [the longest x1 0.1 us: tables(): mine = lax.dynamic_slice(shifts, (0, 0, lat * br, lon * bc), (STEPS, 3, b...]
    transpose x6 -> x0, local copies, waits for them, and re-layouts: 9.74 us -> none  [the longest x2 8.02 us: interpolate(): jnp.einsum('nlm,nimt->nilt', weight_z, stacked, precision=lax.Precision.H...]
    slice x18 -> x2, local copies, waits for them, and re-layouts: 4.64 us -> 0.08 us  [the longest x1 0.07 us: tables(): w0 = area - 2.0 * ka + jnp.pad(ka[1:], (0, 1)) + jnp.pad(ka[:-1], (1, 0))]
    unnamed x64 -> x13, local copies, waits for them, and re-layouts: 0.13 us -> 4.63 us
  transfers between devices with their start and end apart: 16 -> 0, of which waited for: 3 -> 0; matrix products, arithmetic and copies ran while one was open for 28% -> 0% of each run, Pallas kernels for 0% -> 0%
where the time goes in v1:
time: 40.5 us; the launch traced here: 40.3 us
  Pallas kernels  31.9 us (79%)
  local copies, waits for them, and re-layouts  7.03 us (17%)
  other arithmetic  1.23 us (3%)
    pallas_call x1, Pallas kernels, local(): pl.pallas_call(functools.partial(kernel, br, bc, lats, lons), out_shape=j...  31.9 us
    unnamed x13, local copies, waits for them, and re-layouts  4.63 us

profile of v1, /device:TPU:0, one launch (start us, length us, event | category | flops | bytes accessed | tf_op | source)
XLA Modules:
  0.0 40.3 jit_solution(10679138266741634972)
XLA Ops:
  0.0 0.7 %copy-done.3 = f32[32]{0:T(128)S(1)} copy-done((f32[32]{0:T(128)S(1)}, f32[32]{0:T(128)}, u32[]{:S(2)}) %copy-start.3) | copy-done | bytes 152
  0.7 0.1 fusion.8
  0.8 0.1 pad_add_fusion.1
  0.9 0.7 %copy-done.5 = s32[4]{0:T(128)S(1)} copy-done((s32[4]{0:T(128)S(1)}, s32[4]{0:T(128)}, u32[]{:S(2)}) %copy-start.5) | copy-done | bytes 40
  1.6 0.1 constant_dynamic-slice_fusion
  1.6 0.1 reshape.151
  1.7 0.1 pad_maximum_fusion.tf
  1.8 0.4 %copy-done.2 = s32[2,16,32]{2,1,0:T(8,128)S(1)} copy-done((s32[2,16,32]{2,1,0:T(8,128)S(1)}, s32[2,16,32]{2,1,0:T(8,128)}, u32[]{:S(2)}) %copy-start.2) | copy-done | bytes 4120
  2.3 0.1 pad_dynamic-slice_fusion
  2.4 0.1 reshape.147
  2.5 0.6 %copy-done.4 = s32[4]{0:T(128)S(1)} copy-done((s32[4]{0:T(128)S(1)}, s32[4]{0:T(128)}, u32[]{:S(2)}) %copy-start.4) | copy-done | bytes 40
  3.2 0.6 %gather_fusion = s32[4,2,32]{2,1,0:T(2,128)S(1)} fusion(s32[2,5,32]{2,0,1:T(2,128)S(1)} %and_select_fusion.2, s32[1024]{0:T(1024)S(1)} %pad_clamp_fusion), kind=kCustom, calls=%fused_computation | custom fusion | bytes 2064 | tf_op jit(solution)/shard_map/gather | solution.py:408
  3.8 0.6 %gather_fusion.2 = s32[4,2,32]{2,1,0:T(2,128)S(1)} fusion(s32[2,5,32]{2,0,1:T(2,128)S(1)} %get-tuple-element.5, s32[1024]{0:T(1024)S(1)} %pad_clamp_fusion), kind=kCustom, calls=%fused_computation.2 | custom fusion | bytes 2064 | tf_op jit(solution)/shard_map/gather | solution.py:410
  4.4 0.3 convert_reduce_fusion
  4.8 0.6 %gather_fusion.1 = s32[4,2,32]{2,1,0:T(2,128)S(1)} fusion(s32[2,5,32]{2,0,1:T(2,128)S(1)} %copy.37, s32[1024]{0:T(1024)S(1)} %pad_clamp_fusion), kind=kCustom, calls=%fused_computation.1 | custom fusion | bytes 2064 | tf_op jit(solution)/shard_map/gather | solution.py:409
  5.4 0.2 select_reduce_fusion.1
  5.6 0.1 reshape.148
  5.7 0.2 select_reduce_fusion
  5.9 0.1 reshape.149
  6.0 0.1 pad_add_fusion
  6.1 0.1 reshape.150.ti
  6.2 1.2 %copy-done.1 = f32[32,64,128]{2,1,0:T(8,128)S(1)} copy-done((f32[32,64,128]{2,1,0:T(8,128)S(1)}, f32[32,64,128]{2,1,0:T(8,128)}, u32[]{:S(2)}) %copy-start.1) | copy-done | bytes 1048600
  7.4 31.9 %shard_map.64 = f32[4,8,8,8,128]{4,3,2,1,0:T(8,128)S(1)} custom-call(s32[192]{0:T(256)S(1)} %reshape.150.ti, f32[288]{0:T(512)S(1)} %pad_maximum_fusion.tf, f32[4,8,8,8,128]{4,3,2,1,0:T(8,128)S(1)} %bitcast.23), custom_call_target="tpu_custom_call" | custom-call | tf_op jit(solution)/shard_map/pallas_call | solution.py:440
  39.3 1.0 %copy.48 = f32[32,64,128]{2,1,0:T(8,128)} copy(f32[32,64,128]{2,1,0:T(8,128)S(1)} %bitcast.22) | data formatting | bytes 2097152
  (23 shorter events, 0.3 us)
Async XLA Ops:
  0.0 1.5 %copy-start = (f32[2,3,16,32]{3,2,1,0:T(8,128)S(1)}, f32[2,3,16,32]{3,2,1,0:T(8,128)}, u32[]{:S(2)}) copy-start(f32[2,3,16,32]{3,2,1,0:T(8,128)} %param.7) | copy-start | bytes 36868
  0.0 0.7 %copy-start.3 = (f32[32]{0:T(128)S(1)}, f32[32]{0:T(128)}, u32[]{:S(2)}) copy-start(f32[32]{0:T(128)} %param.8) | copy-start | bytes 388
  0.9 0.7 %copy-start.5 = (s32[4]{0:T(128)S(1)}, s32[4]{0:T(128)}, u32[]{:S(2)}) copy-start(s32[4]{0:T(128)} %constant.95) | copy-start | bytes 52
  1.6 0.7 %copy-start.2 = (s32[2,16,32]{2,1,0:T(8,128)S(1)}, s32[2,16,32]{2,1,0:T(8,128)}, u32[]{:S(2)}) copy-start(s32[2,16,32]{2,1,0:T(8,128)} %param.9) | copy-start | bytes 12292
  2.5 0.7 %copy-start.4 = (s32[4]{0:T(128)S(1)}, s32[4]{0:T(128)}, u32[]{:S(2)}) copy-start(s32[4]{0:T(128)} %constant.84.clone) | copy-start | bytes 52
  6.2 1.2 %copy-start.1 = (f32[32,64,128]{2,1,0:T(8,128)S(1)}, f32[32,64,128]{2,1,0:T(8,128)}, u32[]{:S(2)}) copy-start(f32[32,64,128]{2,1,0:T(8,128)} %param.6) | copy-start | bytes 3145732

commit v2 on v1

--- a/solution.py
+++ b/solution.py
@@ -79,11 +79,20 @@
     return done
 
 
+def several(count, unroll, body, carry):
+    def turn(i, carry):
+        for k in range(unroll):
+            carry = body(i * unroll + k, carry)
+        return carry
+
+    return lax.fori_loop(0, count // unroll, turn, carry)
+
+
 def kernel(
     br, bc, lats, lons,
     ti, tf, tr, out,
-    st, arr, ia, snd, adv, outbuf, side_out, side_in, ka_out, ka_in, mass_out, mass_in,
-    load_sem, store_sem, psend, precv, hsend, hrecv, ksend, krecv, msend, mrecv,
+    st, arr, ia, snd, adv, side_out, side_in, ka_out, ka_in, mass_out, mass_in,
+    load_sem, psend, precv, hsend, hrecv, ksend, krecv, msend, mrecv,
 ):
     np_ = br * bc
     rows = br * 8
@@ -216,7 +225,7 @@
                 adv[s, c, 1 + r * 8 + i] = done[i]
             return 0
 
-        lax.fori_loop(0, np_, own, 0)
+        several(np_, 4, own, 0)
         for o in (1, 2, 0, 3):
 
             @pl.when(in_range(OFFSETS[o]))
@@ -233,7 +242,7 @@
                         ia[s, o * CAP + j, i] = done[i]
                     return 0
 
-                lax.fori_loop(0, CAP, come, 0)
+                several(CAP, CAP, come, 0)
 
         def join(q, total):
             c, r = q // br, lax.rem(q, br)
@@ -247,7 +256,7 @@
                 total = total + tf[w0 + r * 8 + i] * v
             return total
 
-        total = lax.fori_loop(0, np_, join, zero)
+        total = several(np_, 4, join, zero)
         for i in range(2):
 
             @pl.when(in_range(2 * i - 1))
@@ -304,7 +313,7 @@
         parts = [st[0, c * br + row // 8, lax.rem(row, 8)] for c in range(bc)]
         return total + tf[area0 + row] * functools.reduce(jnp.add, parts)
 
-    target_part = lax.fori_loop(0, rows, target_row, zero)
+    target_part = several(rows, 4, target_row, zero)
     for i in range(2):
 
         @pl.when(in_range(2 * i - 1))
@@ -330,7 +339,7 @@
             st[1, c * br + row // 8, lax.rem(row, 8)] = done[c]
         return 0
 
-    lax.fori_loop(0, rows, first_step, 0)
+    several(rows, 4, first_step, 0)
     send_patches(1)
     sums = masses_sum(0)
     target = sums[1:2]
@@ -343,19 +352,13 @@
     wait_halos(1)
     ratio = jnp.broadcast_to(target / masses_sum(1)[0:1], (8, values))
 
-    stores = []
-    for r in range(br):
-
-        def last_step(i, _):
-            done = diffused_row(1, r * 8 + i)
-            for c in range(bc):
-                outbuf[r, i, c] = done[c] * ratio
-            return 0
-
-        lax.fori_loop(0, 8, last_step, 0)
-        copy = pltpu.make_async_copy(outbuf.at[r], out.at[r], store_sem.at[r])
-        copy.start()
-        stores.append(copy)
+    def last_step(row, _):
+        done = diffused_row(1, row)
+        for c in range(bc):
+            out[row // 8, lax.rem(row, 8), c] = done[c] * ratio
+        return 0
+
+    several(rows, 4, last_step, 0)
 
     for s in range(STEPS):
         for o in range(4):
@@ -378,9 +381,6 @@
         @pl.when(in_range(2 * i - 1))
         def _():
             ka_copy(i).wait_send()
-
-    for copy in stores:
-        copy.wait()
 
 
 def tables(source_patch, shifts, diffusivity, br, bc, rows):
@@ -439,20 +439,19 @@
     f32 = jnp.float32
     result = pl.pallas_call(
         functools.partial(kernel, br, bc, lats, lons),
-        out_shape=jax.ShapeDtypeStruct((br, 8, bc, 8, values), f32),
+        out_shape=pltpu.VMEM((br, 8, bc, 8, values), f32),
         in_specs=[
             pl.BlockSpec(memory_space=pltpu.SMEM),
             pl.BlockSpec(memory_space=pltpu.SMEM),
-            pl.BlockSpec(memory_space=pl.ANY),
+            pl.BlockSpec(memory_space=pltpu.HBM),
         ],
-        out_specs=pl.BlockSpec(memory_space=pl.ANY),
+        out_specs=pl.BlockSpec(memory_space=pltpu.VMEM),
         scratch_shapes=[
             pltpu.VMEM((STEPS, np_) + tile, f32),
             pltpu.VMEM((STEPS, 4, CAP) + tile, f32),
             pltpu.VMEM((STEPS, 4 * CAP) + tile, f32),
             pltpu.VMEM((STEPS, 4, CAP) + tile, f32),
             pltpu.VMEM((STEPS, bc, rows + 2, 8, values), f32),
-            pltpu.VMEM((br, 8, bc, 8, values), f32),
             pltpu.VMEM((STEPS, 2, rows, values), f32),
             pltpu.VMEM((STEPS, 2, rows, values), f32),
             pltpu.VMEM((2, 1, values), f32),
@@ -460,7 +459,6 @@
             pltpu.VMEM((STEPS, 2, values), f32),
             pltpu.VMEM((STEPS, peers, 2, values), f32),
             dma((bc,)),
-            dma((br,)),
             dma((STEPS, 4)),
             dma((STEPS, 4)),
             dma((STEPS, 4)),

time: 40.5 us -> 37.9 us (0.936)
  Pallas kernels: 31.9 us -> 29.2 us
    pallas_call x1, Pallas kernels: 31.9 us -> 29.2 us  [local(): pl.pallas_call(functools.partial(kernel, br, bc, lats, lons), out_shape=p...]
where the time goes in v2:
time: 37.9 us; the launch traced here: 37.6 us
  Pallas kernels  29.2 us (77%)
  local copies, waits for them, and re-layouts  7.03 us (19%)
  other arithmetic  1.23 us (3%)
    pallas_call x1, Pallas kernels, local(): pl.pallas_call(functools.partial(kernel, br, bc, lats, lons), out_shape=p...  29.2 us
    unnamed x13, local copies, waits for them, and re-layouts  4.63 us

profile of v2, /device:TPU:0, one launch (start us, length us, event | category | flops | bytes accessed | tf_op | source)
XLA Modules:
  0.0 37.6 jit_solution(5041383141641799113)
XLA Ops:
  0.0 0.7 %copy-done.3 = f32[32]{0:T(128)S(1)} copy-done((f32[32]{0:T(128)S(1)}, f32[32]{0:T(128)}, u32[]{:S(2)}) %copy-start.3) | copy-done | bytes 152
  0.7 0.1 fusion.8
  0.8 0.1 pad_add_fusion.1
  0.9 0.7 %copy-done.5 = s32[4]{0:T(128)S(1)} copy-done((s32[4]{0:T(128)S(1)}, s32[4]{0:T(128)}, u32[]{:S(2)}) %copy-start.5) | copy-done | bytes 40
  1.6 0.1 constant_dynamic-slice_fusion
  1.6 0.1 reshape.151
  1.7 0.1 pad_maximum_fusion.tf
  1.8 0.4 %copy-done.2 = s32[2,16,32]{2,1,0:T(8,128)S(1)} copy-done((s32[2,16,32]{2,1,0:T(8,128)S(1)}, s32[2,16,32]{2,1,0:T(8,128)}, u32[]{:S(2)}) %copy-start.2) | copy-done | bytes 4120
  2.3 0.1 pad_dynamic-slice_fusion
  2.4 0.1 reshape.147
  2.5 0.6 %copy-done.4 = s32[4]{0:T(128)S(1)} copy-done((s32[4]{0:T(128)S(1)}, s32[4]{0:T(128)}, u32[]{:S(2)}) %copy-start.4) | copy-done | bytes 40
  3.2 0.6 %gather_fusion = s32[4,2,32]{2,1,0:T(2,128)S(1)} fusion(s32[2,5,32]{2,0,1:T(2,128)S(1)} %and_select_fusion.2, s32[1024]{0:T(1024)S(1)} %pad_clamp_fusion), kind=kCustom, calls=%fused_computation | custom fusion | bytes 2064 | tf_op jit(solution)/shard_map/gather | solution.py:408
  3.8 0.6 %gather_fusion.2 = s32[4,2,32]{2,1,0:T(2,128)S(1)} fusion(s32[2,5,32]{2,0,1:T(2,128)S(1)} %get-tuple-element.5, s32[1024]{0:T(1024)S(1)} %pad_clamp_fusion), kind=kCustom, calls=%fused_computation.2 | custom fusion | bytes 2064 | tf_op jit(solution)/shard_map/gather | solution.py:410
  4.4 0.3 convert_reduce_fusion
  4.8 0.6 %gather_fusion.1 = s32[4,2,32]{2,1,0:T(2,128)S(1)} fusion(s32[2,5,32]{2,0,1:T(2,128)S(1)} %copy.37, s32[1024]{0:T(1024)S(1)} %pad_clamp_fusion), kind=kCustom, calls=%fused_computation.1 | custom fusion | bytes 2064 | tf_op jit(solution)/shard_map/gather | solution.py:409
  5.4 0.2 select_reduce_fusion.1
  5.6 0.1 reshape.148
  5.7 0.2 select_reduce_fusion
  5.9 0.1 reshape.149
  6.0 0.1 pad_add_fusion
  6.1 0.1 reshape.150.ti
  6.2 1.2 %copy-done.1 = f32[32,64,128]{2,1,0:T(8,128)S(1)} copy-done((f32[32,64,128]{2,1,0:T(8,128)S(1)}, f32[32,64,128]{2,1,0:T(8,128)}, u32[]{:S(2)}) %copy-start.1) | copy-done | bytes 1048600
  7.4 29.2 %shard_map.64 = f32[4,8,8,8,128]{4,3,2,1,0:T(8,128)S(1)} custom-call(s32[192]{0:T(256)S(1)} %reshape.150.ti, f32[288]{0:T(512)S(1)} %pad_maximum_fusion.tf, f32[4,8,8,8,128]{4,3,2,1,0:T(8,128)S(1)} %bitcast.23), custom_call_target="tpu_custom_call" | custom-call | tf_op jit(solution)/shard_map/pallas_call | solution.py:440
  36.6 1.0 %copy.48 = f32[32,64,128]{2,1,0:T(8,128)} copy(f32[32,64,128]{2,1,0:T(8,128)S(1)} %bitcast.22) | data formatting | bytes 2097152
  (23 shorter events, 0.3 us)
Async XLA Ops:
  0.0 1.5 %copy-start = (f32[2,3,16,32]{3,2,1,0:T(8,128)S(1)}, f32[2,3,16,32]{3,2,1,0:T(8,128)}, u32[]{:S(2)}) copy-start(f32[2,3,16,32]{3,2,1,0:T(8,128)} %param.7) | copy-start | bytes 36868
  0.0 0.7 %copy-start.3 = (f32[32]{0:T(128)S(1)}, f32[32]{0:T(128)}, u32[]{:S(2)}) copy-start(f32[32]{0:T(128)} %param.8) | copy-start | bytes 388
  0.9 0.7 %copy-start.5 = (s32[4]{0:T(128)S(1)}, s32[4]{0:T(128)}, u32[]{:S(2)}) copy-start(s32[4]{0:T(128)} %constant.95) | copy-start | bytes 52
  1.6 0.7 %copy-start.2 = (s32[2,16,32]{2,1,0:T(8,128)S(1)}, s32[2,16,32]{2,1,0:T(8,128)}, u32[]{:S(2)}) copy-start(s32[2,16,32]{2,1,0:T(8,128)} %param.9) | copy-start | bytes 12292
  2.5 0.7 %copy-start.4 = (s32[4]{0:T(128)S(1)}, s32[4]{0:T(128)}, u32[]{:S(2)}) copy-start(s32[4]{0:T(128)} %constant.84.clone) | copy-start | bytes 52
  6.2 1.2 %copy-start.1 = (f32[32,64,128]{2,1,0:T(8,128)S(1)}, f32[32,64,128]{2,1,0:T(8,128)}, u32[]{:S(2)}) copy-start(f32[32,64,128]{2,1,0:T(8,128)} %param.6) | copy-start | bytes 3145732

commit v3 on v2

--- a/solution.py
+++ b/solution.py
@@ -14,13 +14,6 @@
 OFFSETS = (-2, -1, 1, 2)
 SENT_FIRST = (0, 3, 1, 2)
 MESH = pl.DeviceIdType.MESH
-
-
-def column_area(first_row, row_count, total_rows):
-    latitude = ((first_row + jnp.arange(row_count)).astype(jnp.float32) + 0.5) * (
-        math.pi / total_rows
-    ) - 0.5 * math.pi
-    return jnp.cos(latitude)
 
 
 def cubic_weights(s):
@@ -42,13 +35,15 @@
     )
 
 
-def interpolate(rows, fractions, ratio):
+def interpolate(rows, weights, ratio):
     values = rows[0].shape[1]
     step = values // LEV
     column = lax.broadcasted_iota(jnp.int32, (8, values), 0)
     level = lax.broadcasted_iota(jnp.int32, (8, values), 1) // step
-    sy, sx, sz = (jnp.full((8, values), s, jnp.float32) for s in fractions)
-    a, b, c, d = cubic_weights(sy)
+    wy, wx, wz = (
+        [jnp.full((8, values), w, jnp.float32) for w in part] for part in weights
+    )
+    a, b, c, d = wy
     ab, cd = a + b, c + d
     bcd = b + cd
     x = rows
@@ -59,8 +54,8 @@
         out.append(a * x[i - 1] + b * x[i] + c * x[i + 1] + d * x[i + 2])
     out.append(a * x[5] + b * x[6] + cd * x[7])
     out.append(a * x[6] + bcd * x[7])
-    wx = place_weights(cubic_weights(sx), column, 7)
-    wz = place_weights(cubic_weights(sz), level, LEV - 1)
+    wx = place_weights(wx, column, 7)
+    wz = place_weights(wz, level, LEV - 1)
     done = []
     for v in out:
         v = (
@@ -79,6 +74,108 @@
     return done
 
 
+def quotient(x, n):
+    if n & (n - 1) == 0:
+        return lax.shift_right_logical(x, jnp.full_like(x, n.bit_length() - 1))
+    return lax.div(x, jnp.full_like(x, n))
+
+
+def make_tables(br, bc, lats, lat, lon, source, shift, near, near_shift, ti, tf):
+    np_ = br * bc
+    rows = br * 8
+    lat_rows, total_cols = source.shape[1:]
+    lanes = ti.shape[1]
+    lane = lax.broadcasted_iota(jnp.int32, (8, lanes), 1)
+    sub = lax.broadcasted_iota(jnp.int32, (8, lanes), 0)
+    at = lax.broadcasted_iota(jnp.int32, (total_cols, lanes), 0)
+    entry = lax.broadcasted_iota(jnp.int32, (total_cols, lanes), 1)
+    pick_columns = jnp.where(at == lon * bc + entry % bc, 1.0, 0.0)
+    near[...] = jnp.dot(
+        source[...].reshape(STEPS * lat_rows, total_cols).astype(jnp.float32),
+        pick_columns,
+        precision=lax.Precision.HIGHEST,
+        preferred_element_type=jnp.float32,
+    )
+    near_shift[...] = jnp.dot(
+        shift[...].reshape(STEPS * 3 * lat_rows, total_cols),
+        pick_columns,
+        precision=lax.Precision.HIGHEST,
+        preferred_element_type=jnp.float32,
+    )
+    row_of = lax.broadcasted_iota(jnp.int32, (br, lanes), 1) // bc
+    own_row = row_of == lax.broadcasted_iota(jnp.int32, (br, lanes), 0)
+
+    def band(ref, first):
+        block = ref[pl.ds(first, br), :]
+        return jnp.sum(jnp.where(own_row, block, 0.0), axis=0, keepdims=True)
+
+    parts = [band(near_shift, k * lat_rows + lat * br) for k in range(STEPS * 3)]
+    parts += [parts[0]] * (8 - STEPS * 3)
+    for k, w in enumerate(cubic_weights(jnp.concatenate(parts, axis=0))):
+        tf[8 * k : 8 * k + 8, :] = w
+    latitude = ((lat * rows + lane).astype(jnp.float32) + 0.5) * (
+        math.pi / (rows * lats)
+    ) - 0.5 * math.pi
+    tf[32:40, :] = jnp.cos(latitude)
+
+    valid = lane < np_
+    dest = jnp.clip(lat + jnp.minimum(sub, 4) - 2, 0, lats - 1)
+    own_rows = []
+    for s in range(STEPS):
+        places = [
+            s * lat_rows + jnp.clip(lat + o, 0, lats - 1) * br for o in range(-2, 3)
+        ]
+        bands = [band(near, p) for p in places]
+        bands += [bands[4]] * 3
+        ids = jnp.concatenate(bands, axis=0).astype(jnp.int32)
+        source_row = quotient(ids, total_cols)
+        source_dev = quotient(source_row, br)
+        source_q = (ids - source_row * total_cols - lon * bc) * br + (
+            source_row - source_dev * br
+        )
+        relative = source_dev - dest + 2
+        count = jnp.zeros((8, lanes), jnp.int32)
+        for k in range(5):
+            count = jnp.where((relative == k) & valid, 1 << (6 * k), count)
+        reach = 1
+        while reach < np_:
+            count = count + jnp.where(lane >= reach, pltpu.roll(count, reach, 1), 0)
+            reach *= 2
+        rank = jnp.zeros((8, lanes), jnp.int32)
+        for k in range(5):
+            field = lax.shift_right_logical(count, jnp.full_like(count, 6 * k))
+            rank = jnp.where(relative == k, (field & 63) - 1, rank)
+        code = jnp.where((source_dev == lat) & valid, rank, -1)
+
+        def spread(x, picks):
+            return jnp.concatenate(
+                [jnp.broadcast_to(x[p : p + 1], (CAP, lanes)) for p in picks], axis=0
+            )
+
+        outer = (0, 1, 3, 4)
+        slot = lax.broadcasted_iota(jnp.int32, (4 * CAP, lanes), 0)
+        which = slot // CAP
+        which = jnp.where(which >= 2, which + 1, which)
+        slot = slot % CAP
+        place = lax.broadcasted_iota(jnp.int32, (4 * CAP, lanes), 1)
+        sent = jnp.where(spread(code, outer) == slot, spread(source_q, outer), 0)
+        mine = (2,) * 4
+        hit = (spread(relative, mine) == which) & (spread(rank, mine) == slot)
+        come = jnp.where(hit & (place < np_), place, 0)
+        sent = jnp.sum(sent.astype(jnp.float32), axis=1, keepdims=True)
+        come = jnp.sum(come.astype(jnp.float32), axis=1, keepdims=True)
+        ti[s * 4 * CAP : (s + 1) * 4 * CAP, :] = jnp.clip(
+            jnp.where(place == 0, sent, come).astype(jnp.int32), 0, np_ - 1
+        )
+        here = relative == 2
+        outer_place = jnp.where(relative > 2, relative - 1, relative) * CAP + rank
+        own_rows.append(jnp.clip(jnp.where(here & valid, source_q, 0), 0, np_ - 1)[2:3])
+        outer_place = jnp.clip(outer_place, 0, 4 * CAP - 1)
+        own_rows.append(jnp.where(here | ~valid, -1, outer_place)[2:3])
+    own_rows += own_rows[:1] * (8 - len(own_rows))
+    ti[STEPS * 4 * CAP :, :] = jnp.concatenate(own_rows, axis=0)
+
+
 def several(count, unroll, body, carry):
     def turn(i, carry):
         for k in range(unroll):
@@ -90,9 +187,10 @@
 
 def kernel(
     br, bc, lats, lons,
-    ti, tf, tr, out,
+    source_hbm, shift_hbm, kappa_hbm, tr, out,
     st, arr, ia, snd, adv, side_out, side_in, ka_out, ka_in, mass_out, mass_in,
-    load_sem, psend, precv, hsend, hrecv, ksend, krecv, msend, mrecv,
+    source, shift, near, near_shift, ti_v, tf_v, ti, tf, kappa, weight,
+    load_sem, small_sem, psend, precv, hsend, hrecv, ksend, krecv, msend, mrecv,
 ):
     np_ = br * bc
     rows = br * 8
@@ -100,12 +198,14 @@
     values = tr.shape[-1]
     lat = lax.axis_index("lat")
     lon = lax.axis_index("lon")
-    kappa0 = STEPS * 3 * np_
-    area0 = kappa0 + rows
-    w0 = area0 + rows
-    send0, arrive0, local0, pick0 = 0, 4 * CAP, 8 * CAP, 8 * CAP + np_
-    per_step = 8 * CAP + 2 * np_
-
+
+    small = [
+        pltpu.make_async_copy(source_hbm, source, small_sem.at[0]),
+        pltpu.make_async_copy(shift_hbm, shift, small_sem.at[1]),
+        pltpu.make_async_copy(kappa_hbm, kappa, small_sem.at[2]),
+    ]
+    for copy in small:
+        copy.start()
     loads = [
         pltpu.make_async_copy(
             tr.at[:, :, c], st.at[0, pl.ds(c * br, br)], load_sem.at[c]
@@ -121,10 +221,6 @@
             adv[s, c, 0] = zero
             adv[s, c, rows + 1] = zero
     ka_in[...] = jnp.zeros_like(ka_in)
-    ka_out[0] = jnp.full((1, values), tf[kappa0] * tf[area0], jnp.float32)
-    ka_out[1] = jnp.full(
-        (1, values), tf[kappa0 + rows - 1] * tf[area0 + rows - 1], jnp.float32
-    )
 
     def peer(k):
         return {
@@ -139,6 +235,25 @@
         return 0
 
     lax.fori_loop(1, peers, greet, 0)
+    for copy in small:
+        copy.wait()
+    make_tables(
+        br, bc, lats, lat, lon, source, shift, near, near_shift, ti_v, tf_v
+    )
+    to_scalar = [
+        pltpu.make_async_copy(ti_v, ti, small_sem.at[3]),
+        pltpu.make_async_copy(tf_v, tf, small_sem.at[4]),
+    ]
+    for copy in to_scalar:
+        copy.start()
+    for copy in to_scalar:
+        copy.wait()
+
+    def area(row):
+        return tf[32, row]
+
+    for i, row in enumerate((0, rows - 1)):
+        ka_out[i] = jnp.full((1, values), kappa[row] * area(row), jnp.float32)
     pl.semaphore_wait(barrier, peers - 1)
 
     def in_range(offset):
@@ -187,14 +302,14 @@
     def send_patches(s):
         for o in SENT_FIRST:
             for j in range(CAP):
-                snd[s, o, j] = st[s, ti[s * per_step + send0 + o * CAP + j]]
+                snd[s, o, j] = st[s, ti[(s * 4 + o) * CAP + j, 0]]
 
             @pl.when(in_range(OFFSETS[o]))
             def _():
                 patch_copy(s, o).start()
 
-    def fractions(s, e):
-        return tuple(tf[(s * 3 + i) * np_ + e] for i in range(3))
+    def weights(s, e):
+        return [[tf[8 * k + s * 3 + i, e] for k in range(4)] for i in range(3)]
 
     def masses(s):
         def send(k, _):
@@ -219,8 +334,8 @@
         def own(q, _):
             c, r = q // br, lax.rem(q, br)
             e = r * bc + c
-            block = st[s, ti[s * per_step + local0 + e]]
-            done = interpolate([block[i] for i in range(8)], fractions(s, e), ratio)
+            block = st[s, ti[STEPS * 4 * CAP + 2 * s, e]]
+            done = interpolate([block[i] for i in range(8)], weights(s, e), ratio)
             for i in range(8):
                 adv[s, c, 1 + r * 8 + i] = done[i]
             return 0
@@ -233,10 +348,10 @@
                 patch_copy(s, 3 - o).wait_recv()
 
                 def come(j, _):
-                    e = ti[s * per_step + arrive0 + o * CAP + j]
+                    e = ti[(s * 4 + o) * CAP + j, 1]
                     block = arr[s, o, j]
                     done = interpolate(
-                        [block[i] for i in range(8)], fractions(s, e), ratio
+                        [block[i] for i in range(8)], weights(s, e), ratio
                     )
                     for i in range(8):
                         ia[s, o * CAP + j, i] = done[i]
@@ -247,13 +362,13 @@
         def join(q, total):
             c, r = q // br, lax.rem(q, br)
             e = r * bc + c
-            pick = ti[s * per_step + pick0 + e]
+            pick = ti[STEPS * 4 * CAP + 2 * s + 1, e]
             block = ia[s, jnp.maximum(pick, 0)]
             far = jnp.full((8, values), pick, jnp.int32) >= 0
             for i in range(8):
                 v = jnp.where(far, block[i], adv[s, c, 1 + r * 8 + i])
                 adv[s, c, 1 + r * 8 + i] = v
-                total = total + tf[w0 + r * 8 + i] * v
+                total = total + weight[r * 8 + i] * v
             return total
 
         total = several(np_, 4, join, zero)
@@ -289,13 +404,13 @@
         behind = [pltpu.roll(v, 1, 0) for v in here]
         west = jnp.broadcast_to(side_in[s, 0, pl.ds(row, 1)], (8, values))
         east = jnp.broadcast_to(side_in[s, 1, pl.ds(row, 1)], (8, values))
-        kappa = tf[kappa0 + row]
+        number = kappa[row]
         result = []
         for c in range(bc):
             e = jnp.where(column == 7, east if c == bc - 1 else ahead[c + 1], ahead[c])
             w = jnp.where(column == 0, west if c == 0 else behind[c - 1], behind[c])
             lap = adv[s, c, row] + adv[s, c, row + 2] + e + w - 4.0 * here[c]
-            result.append(here[c] + kappa * lap)
+            result.append(here[c] + number * lap)
         return result
 
     for i in range(2):
@@ -309,9 +424,17 @@
 
     send_patches(0)
 
+    for row in range(rows):
+        w = area(row) * (1.0 - 2.0 * kappa[row])
+        if row:
+            w = w + area(row - 1) * kappa[row - 1]
+        if row < rows - 1:
+            w = w + area(row + 1) * kappa[row + 1]
+        weight[row] = w
+
     def target_row(row, total):
         parts = [st[0, c * br + row // 8, lax.rem(row, 8)] for c in range(bc)]
-        return total + tf[area0 + row] * functools.reduce(jnp.add, parts)
+        return total + area(row) * functools.reduce(jnp.add, parts)
 
     target_part = several(rows, 4, target_row, zero)
     for i in range(2):
@@ -383,56 +506,10 @@
             ka_copy(i).wait_send()
 
 
-def tables(source_patch, shifts, diffusivity, br, bc, rows):
-    lats = lax.axis_size("lat")
-    lat = lax.axis_index("lat")
-    lon = lax.axis_index("lon")
-    np_ = br * bc
-    total_cols = source_patch.shape[2]
-    padded = jnp.pad(
-        source_patch, ((0, 0), (2 * br, 2 * br), (0, 0)), constant_values=-1
-    )
-    near = lax.dynamic_slice(
-        padded, (0, lat * br, lon * bc), (STEPS, 5 * br, bc)
-    ).reshape(STEPS, 5, np_)
-    source_row = near // total_cols
-    source_dev = source_row // br
-    source_q = (near % total_cols - lon * bc) * br + source_row % br
-    entries = jnp.arange(np_)
-    earlier = entries[None, :] < entries[:, None]
-    same = source_dev[..., :, None] == source_dev[..., None, :]
-    rank = jnp.sum((same & earlier).astype(jnp.int32), axis=-1)
-    outer = jnp.array([0, 1, 3, 4])
-    relative = source_dev[:, 2] - lat
-    slots = jnp.arange(CAP)
-    from_here = source_dev[:, outer] == lat
-    chosen = from_here[..., None] & (rank[:, outer][..., None] == slots)
-    send = jnp.sum(jnp.where(chosen, source_q[:, outer][..., None], 0), axis=2)
-    arrives = relative[:, None, :] == jnp.array(OFFSETS)[None, :, None]
-    chosen = arrives[..., None] & (rank[:, 2][:, None, :, None] == slots)
-    arrive = jnp.sum(jnp.where(chosen, entries[None, None, :, None], 0), axis=2)
-    is_local = relative == 0
-    local = jnp.where(is_local, source_q[:, 2], 0)
-    place = jnp.where(relative < 0, relative + 2, relative + 1) * CAP + rank[:, 2]
-    pick = jnp.where(is_local, -1, place)
-    ti = jnp.concatenate(
-        [send.reshape(STEPS, -1), arrive.reshape(STEPS, -1), local, pick], axis=1
-    ).reshape(-1)
-    mine = lax.dynamic_slice(
-        shifts, (0, 0, lat * br, lon * bc), (STEPS, 3, br, bc)
-    ).reshape(-1)
-    area = column_area(lat * rows, rows, rows * lats)
-    ka = diffusivity * area
-    w0 = area - 2.0 * ka + jnp.pad(ka[1:], (0, 1)) + jnp.pad(ka[:-1], (1, 0))
-    tf = jnp.concatenate([mine, diffusivity, area, w0])
-    return ti.astype(jnp.int32), tf
-
-
 def local(lats, lons, tracers, shifts, diffusivity, source_patch):
     rows, cols, values = tracers.shape
     br, bc = rows // 8, cols // 8
     np_ = br * bc
-    ti, tf = tables(source_patch, shifts, diffusivity, br, bc, rows)
     tile = (8, 8, values)
     peers = lats * lons
     dma = pltpu.SemaphoreType.DMA
@@ -441,8 +518,9 @@
         functools.partial(kernel, br, bc, lats, lons),
         out_shape=pltpu.VMEM((br, 8, bc, 8, values), f32),
         in_specs=[
-            pl.BlockSpec(memory_space=pltpu.SMEM),
-            pl.BlockSpec(memory_space=pltpu.SMEM),
+            pl.BlockSpec(memory_space=pltpu.HBM),
+            pl.BlockSpec(memory_space=pltpu.HBM),
+            pl.BlockSpec(memory_space=pltpu.HBM),
             pl.BlockSpec(memory_space=pltpu.HBM),
         ],
         out_specs=pl.BlockSpec(memory_space=pltpu.VMEM),
@@ -458,7 +536,18 @@
             pltpu.VMEM((2, 1, values), f32),
             pltpu.VMEM((STEPS, 2, values), f32),
             pltpu.VMEM((STEPS, peers, 2, values), f32),
+            pltpu.VMEM(source_patch.shape, jnp.int32),
+            pltpu.VMEM(shifts.shape, f32),
+            pltpu.VMEM((STEPS * source_patch.shape[1], 128), f32),
+            pltpu.VMEM((STEPS * 3 * source_patch.shape[1], 128), f32),
+            pltpu.VMEM((STEPS * 4 * CAP + 8, 128), jnp.int32),
+            pltpu.VMEM((40, 128), f32),
+            pltpu.SMEM((STEPS * 4 * CAP + 8, 128), jnp.int32),
+            pltpu.SMEM((40, 128), f32),
+            pltpu.SMEM((rows,), f32),
+            pltpu.SMEM((rows,), f32),
             dma((bc,)),
+            dma((5,)),
             dma((STEPS, 4)),
             dma((STEPS, 4)),
             dma((STEPS, 4)),
@@ -471,7 +560,17 @@
         compiler_params=pltpu.CompilerParams(
             collective_id=0, has_side_effects=True, vmem_limit_bytes=32 * 1024 * 1024
         ),
-    )(ti, tf, tracers.reshape(br, 8, bc, 8, values))
+    )(
+        *(
+            pltpu.with_memory_space_constraint(x, pltpu.HBM)
+            for x in (
+                source_patch,
+                shifts,
+                diffusivity,
+                tracers.reshape(br, 8, bc, 8, values),
+            )
+        )
+    )
     return result.reshape(rows, cols, values)
 
 

time: 37.9 us -> 29.9 us (0.79)
  local copies, waits for them, and re-layouts: 7.03 us -> 0.97 us
  other arithmetic: 1.23 us -> 0 us
  Pallas kernels: 29.2 us -> 28.8 us
    unnamed x13 -> x1, local copies, waits for them, and re-layouts: 4.63 us -> 0.97 us
    gather x5 -> x0, local copies, waits for them, and re-layouts: 1.72 us -> none  [the longest x2 0.58 us: tables(): send = jnp.sum(jnp.where(chosen, source_q[:, outer][..., None], 0), axis=2)]
    reduce_sum x3 -> x0, other arithmetic: 0.79 us -> none  [the longest x1 0.34 us: tables(): rank = jnp.sum((same & earlier).astype(jnp.int32), axis=-1)]
    pallas_call x1, Pallas kernels: 29.2 us -> 28.8 us  [local(): pl.pallas_call(functools.partial(kernel, br, bc, lats, lons), out_shape=p...]
    reshape x5 -> x0, local copies, waits for them, and re-layouts: 0.43 us -> none  [the longest x1 0.1 us: tables(): mine = lax.dynamic_slice(shifts, (0, 0, lat * br, lon * bc), (STEPS, 3, b...]
where the time goes in v3:
time: 29.9 us; the launch traced here: 29.7 us
  Pallas kernels  28.8 us (96%)
  local copies, waits for them, and re-layouts  0.97 us (3%)
    pallas_call x1, Pallas kernels, local(): pl.pallas_call(functools.partial(kernel, br, bc, lats, lons), out_shape=p...  28.8 us
    unnamed x1, local copies, waits for them, and re-layouts  0.97 us

profile of v3, /device:TPU:0, one launch (start us, length us, event | category | flops | bytes accessed | tf_op | source)
XLA Modules:
  0.0 29.7 jit_solution(16625948835658630294)
XLA Ops:
  0.0 28.8 %shard_map.46 = f32[4,8,8,8,128]{4,3,2,1,0:T(8,128)S(1)} custom-call(s32[2,16,32]{2,1,0:T(8,128)} %source_hbm.1, f32[2,3,16,32]{3,2,1,0:T(8,128)} %shift_hbm.1, f32[32]{0:T(128)} %kappa_hbm.1, f32[4,8,8,8,128]{4,3,2,1,0:T(8,128)} %bitcast.3), custom_call_target="tpu_custom_call" | custom-call | tf_op jit(solution)/shard_map/pallas_call | solution.py:517
  28.8 1.0 %copy.6 = f32[32,64,128]{2,1,0:T(8,128)} copy(f32[32,64,128]{2,1,0:T(8,128)S(1)} %bitcast.2) | data formatting | bytes 2097152

commit v4 on v3

--- a/solution.py
+++ b/solution.py
@@ -13,6 +13,8 @@
 CAP = 4
 OFFSETS = (-2, -1, 1, 2)
 SENT_FIRST = (0, 3, 1, 2)
+PIECES = 2
+PIECE = CAP // PIECES
 MESH = pl.DeviceIdType.MESH
 
 
@@ -163,6 +165,8 @@
         hit = (spread(relative, mine) == which) & (spread(rank, mine) == slot)
         come = jnp.where(hit & (place < np_), place, 0)
         sent = jnp.sum(sent.astype(jnp.float32), axis=1, keepdims=True)
+        if s == 0:
+            first_sent = jnp.clip(sent.astype(jnp.int32), 0, np_ - 1)
         come = jnp.sum(come.astype(jnp.float32), axis=1, keepdims=True)
         ti[s * 4 * CAP : (s + 1) * 4 * CAP, :] = jnp.clip(
             jnp.where(place == 0, sent, come).astype(jnp.int32), 0, np_ - 1
@@ -174,6 +178,7 @@
         own_rows.append(jnp.where(here | ~valid, -1, outer_place)[2:3])
     own_rows += own_rows[:1] * (8 - len(own_rows))
     ti[STEPS * 4 * CAP :, :] = jnp.concatenate(own_rows, axis=0)
+    return first_sent
 
 
 def several(count, unroll, body, carry):
@@ -188,7 +193,7 @@
 def kernel(
     br, bc, lats, lons,
     source_hbm, shift_hbm, kappa_hbm, tr, out,
-    st, arr, ia, snd, adv, side_out, side_in, ka_out, ka_in, mass_out, mass_in,
+    st, arr, ia, snd, adv, row_in, side_out, side_in, ka_out, ka_in, mass_out, mass_in,
     source, shift, near, near_shift, ti_v, tf_v, ti, tf, kappa, weight,
     load_sem, small_sem, psend, precv, hsend, hrecv, ksend, krecv, msend, mrecv,
 ):
@@ -221,6 +226,7 @@
             adv[s, c, 0] = zero
             adv[s, c, rows + 1] = zero
     ka_in[...] = jnp.zeros_like(ka_in)
+    row_in[...] = jnp.zeros_like(row_in)
 
     def peer(k):
         return {
@@ -237,7 +243,7 @@
     lax.fori_loop(1, peers, greet, 0)
     for copy in small:
         copy.wait()
-    make_tables(
+    first_sent = make_tables(
         br, bc, lats, lat, lon, source, shift, near, near_shift, ti_v, tf_v
     )
     to_scalar = [
@@ -246,25 +252,17 @@
     ]
     for copy in to_scalar:
         copy.start()
-    for copy in to_scalar:
-        copy.wait()
-
-    def area(row):
-        return tf[32, row]
-
-    for i, row in enumerate((0, rows - 1)):
-        ka_out[i] = jnp.full((1, values), kappa[row] * area(row), jnp.float32)
     pl.semaphore_wait(barrier, peers - 1)
 
     def in_range(offset):
         return (lat + offset >= 0) & (lat + offset < lats)
 
-    def patch_copy(s, o):
+    def patch_copy(s, o, h):
         return pltpu.make_async_remote_copy(
-            src_ref=snd.at[s, o],
-            dst_ref=arr.at[s, 3 - o],
-            send_sem=psend.at[s, o],
-            recv_sem=precv.at[s, 3 - o],
+            src_ref=snd.at[s, o, pl.ds(h * PIECE, PIECE)],
+            dst_ref=arr.at[s, 3 - o, pl.ds(h * PIECE, PIECE)],
+            send_sem=psend.at[s, o, h],
+            recv_sem=precv.at[s, 3 - o, h],
             device_id={"lat": jnp.clip(lat + OFFSETS[o], 0, lats - 1), "lon": lon},
             device_id_type=MESH,
         )
@@ -282,7 +280,7 @@
     def row_copy(s, i):
         return pltpu.make_async_remote_copy(
             src_ref=adv.at[s, :, rows if i else 1],
-            dst_ref=adv.at[s, :, 0 if i else rows + 1],
+            dst_ref=row_in.at[s, 1 - i],
             send_sem=hsend.at[s, i],
             recv_sem=hrecv.at[s, 1 - i],
             device_id={"lat": jnp.clip(lat + 2 * i - 1, 0, lats - 1), "lon": lon},
@@ -299,14 +297,15 @@
             device_id_type=MESH,
         )
 
-    def send_patches(s):
+    def send_patches(s, index):
         for o in SENT_FIRST:
-            for j in range(CAP):
-                snd[s, o, j] = st[s, ti[(s * 4 + o) * CAP + j, 0]]
-
-            @pl.when(in_range(OFFSETS[o]))
-            def _():
-                patch_copy(s, o).start()
+            for h in range(PIECES):
+                for j in range(h * PIECE, (h + 1) * PIECE):
+                    snd[s, o, j] = st[s, index[o * CAP + j]]
+
+                @pl.when(in_range(OFFSETS[o]))
+                def _():
+                    patch_copy(s, o, h).start()
 
     def weights(s, e):
         return [[tf[8 * k + s * 3 + i, e] for k in range(4)] for i in range(3)]
@@ -341,13 +340,19 @@
             return 0
 
         several(np_, 4, own, 0)
-        for o in (1, 2, 0, 3):
-
-            @pl.when(in_range(OFFSETS[o]))
+        odd = lax.rem(lat, 2)
+
+        def arrivals(t, _):
+            turn, h = t // PIECES, lax.rem(t, PIECES)
+            o = jnp.where(turn == 0, 2 - odd, jnp.where(turn == 3, 1 + odd, 3 * (turn - 1)))
+            offset = o - 2 + jnp.where(o >= 2, 1, 0)
+
+            @pl.when(in_range(offset))
             def _():
-                patch_copy(s, 3 - o).wait_recv()
-
-                def come(j, _):
+                piece = arr.at[s, o, pl.ds(h * PIECE, PIECE)]
+                pltpu.make_async_copy(piece, piece, precv.at[s, o, h]).wait()
+                for k in range(PIECE):
+                    j = h * PIECE + k
                     e = ti[(s * 4 + o) * CAP + j, 1]
                     block = arr[s, o, j]
                     done = interpolate(
@@ -355,9 +360,10 @@
                     )
                     for i in range(8):
                         ia[s, o * CAP + j, i] = done[i]
-                    return 0
-
-                several(CAP, CAP, come, 0)
+
+            return 0
+
+        lax.fori_loop(0, 4 * PIECES, arrivals, 0)
 
         def join(q, total):
             c, r = q // br, lax.rem(q, br)
@@ -398,31 +404,53 @@
 
     column = lax.broadcasted_iota(jnp.int32, (8, values), 0)
 
+    def add_halos(s, place):
+        ref, where = place
+        for i, row in enumerate((0, rows - 1)):
+            for c in range(bc):
+                at = where(row, c)
+                ref[at] = ref[at] + kappa[row] * row_in[s, i, c]
+
+        def sides(row, _):
+            for i, c in enumerate((0, bc - 1)):
+                at = where(row, c)
+                side = jnp.broadcast_to(side_in[s, i, pl.ds(row, 1)], (8, values))
+                side = jnp.where(column == (7 if i else 0), side, 0.0)
+                ref[at] = ref[at] + kappa[row] * side
+            return 0
+
+        several(rows, 8, sides, 0)
+
     def diffused_row(s, row):
         here = [adv[s, c, 1 + row] for c in range(bc)]
         ahead = [pltpu.roll(v, 7, 0) for v in here]
         behind = [pltpu.roll(v, 1, 0) for v in here]
-        west = jnp.broadcast_to(side_in[s, 0, pl.ds(row, 1)], (8, values))
-        east = jnp.broadcast_to(side_in[s, 1, pl.ds(row, 1)], (8, values))
         number = kappa[row]
         result = []
         for c in range(bc):
-            e = jnp.where(column == 7, east if c == bc - 1 else ahead[c + 1], ahead[c])
-            w = jnp.where(column == 0, west if c == 0 else behind[c - 1], behind[c])
+            e = jnp.where(column == 7, 0.0 if c == bc - 1 else ahead[c + 1], ahead[c])
+            w = jnp.where(column == 0, 0.0 if c == 0 else behind[c - 1], behind[c])
             lap = adv[s, c, row] + adv[s, c, row + 2] + e + w - 4.0 * here[c]
             result.append(here[c] + number * lap)
         return result
 
+    for copy in loads:
+        copy.wait()
+    send_patches(0, [first_sent[k, 0] for k in range(4 * CAP)])
+    for copy in to_scalar:
+        copy.wait()
+
+    def area(row):
+        return tf[32, row]
+
+    for i, row in enumerate((0, rows - 1)):
+        ka_out[i] = jnp.full((1, values), kappa[row] * area(row), jnp.float32)
     for i in range(2):
 
         @pl.when(in_range(2 * i - 1))
         def _():
             ka_copy(i).start()
 
-    for copy in loads:
-        copy.wait()
-
-    send_patches(0)
 
     for row in range(rows):
         w = area(row) * (1.0 - 2.0 * kappa[row])
@@ -454,16 +482,20 @@
     mass_out[0] = both
     mass_in[0, 0] = both
     masses(0)
-    wait_halos(0)
+
+    def in_state(row, c):
+        return 1, c * br + row // 8, row % 8 if isinstance(row, int) else lax.rem(row, 8)
 
     def first_step(row, _):
         done = diffused_row(0, row)
         for c in range(bc):
-            st[1, c * br + row // 8, lax.rem(row, 8)] = done[c]
+            st[in_state(row, c)] = done[c]
         return 0
 
     several(rows, 4, first_step, 0)
-    send_patches(1)
+    wait_halos(0)
+    add_halos(0, (st, in_state))
+    send_patches(1, [ti[4 * CAP + k, 0] for k in range(4 * CAP)])
     sums = masses_sum(0)
     target = sums[1:2]
     ratio = jnp.broadcast_to(target / sums[0:1], (8, values))
@@ -472,23 +504,35 @@
     mass_out[1] = both
     mass_in[1, 0] = both
     masses(1)
-    wait_halos(1)
-    ratio = jnp.broadcast_to(target / masses_sum(1)[0:1], (8, values))
+
+    def in_out(row, c):
+        return row // 8, row % 8 if isinstance(row, int) else lax.rem(row, 8), c
 
     def last_step(row, _):
         done = diffused_row(1, row)
         for c in range(bc):
-            out[row // 8, lax.rem(row, 8), c] = done[c] * ratio
+            out[in_out(row, c)] = done[c]
         return 0
 
     several(rows, 4, last_step, 0)
+    wait_halos(1)
+    add_halos(1, (out, in_out))
+    ratio = jnp.broadcast_to(target / masses_sum(1)[0:1], (8, values))
+
+    def scale(row, _):
+        for c in range(bc):
+            out[in_out(row, c)] = out[in_out(row, c)] * ratio
+        return 0
+
+    several(rows, 4, scale, 0)
 
     for s in range(STEPS):
         for o in range(4):
 
             @pl.when(in_range(OFFSETS[o]))
             def _():
-                patch_copy(s, o).wait_send()
+                for h in range(PIECES):
+                    patch_copy(s, o, h).wait_send()
 
         for i in range(2):
 
@@ -530,6 +574,7 @@
             pltpu.VMEM((STEPS, 4 * CAP) + tile, f32),
             pltpu.VMEM((STEPS, 4, CAP) + tile, f32),
             pltpu.VMEM((STEPS, bc, rows + 2, 8, values), f32),
+            pltpu.VMEM((STEPS, 2, bc, 8, values), f32),
             pltpu.VMEM((STEPS, 2, rows, values), f32),
             pltpu.VMEM((STEPS, 2, rows, values), f32),
             pltpu.VMEM((2, 1, values), f32),
@@ -548,8 +593,8 @@
             pltpu.SMEM((rows,), f32),
             dma((bc,)),
             dma((5,)),
-            dma((STEPS, 4)),
-            dma((STEPS, 4)),
+            dma((STEPS, 4, PIECES)),
+            dma((STEPS, 4, PIECES)),
             dma((STEPS, 4)),
             dma((STEPS, 4)),
             dma((2,)),

time: 29.9 us -> 31 us (1.037)
  Pallas kernels: 28.8 us -> 29.9 us
    pallas_call x1, Pallas kernels: 28.8 us -> 29.9 us  [local(): pl.pallas_call(functools.partial(kernel, br, bc, lats, lons), out_shape=p...]
where the time goes in v4:
time: 31 us; the launch traced here: 30.9 us
  Pallas kernels  29.9 us (96%)
  local copies, waits for them, and re-layouts  0.97 us (3%)
    pallas_call x1, Pallas kernels, local(): pl.pallas_call(functools.partial(kernel, br, bc, lats, lons), out_shape=p...  29.9 us
    unnamed x1, local copies, waits for them, and re-layouts  0.97 us

profile of v4, /device:TPU:0, one launch (start us, length us, event | category | flops | bytes accessed | tf_op | source)
XLA Modules:
  0.0 30.9 jit_solution(16995485487944107356)
XLA Ops:
  0.0 29.9 %shard_map.46 = f32[4,8,8,8,128]{4,3,2,1,0:T(8,128)S(1)} custom-call(s32[2,16,32]{2,1,0:T(8,128)} %source_hbm.1, f32[2,3,16,32]{3,2,1,0:T(8,128)} %shift_hbm.1, f32[32]{0:T(128)} %kappa_hbm.1, f32[4,8,8,8,128]{4,3,2,1,0:T(8,128)} %bitcast.3), custom_call_target="tpu_custom_call" | custom-call | tf_op jit(solution)/shard_map/pallas_call | solution.py:561
  29.9 1.0 %copy.6 = f32[32,64,128]{2,1,0:T(8,128)} copy(f32[32,64,128]{2,1,0:T(8,128)S(1)} %bitcast.2) | data formatting | bytes 2097152

commit v5 on v4

--- a/solution.py
+++ b/solution.py
@@ -13,7 +13,7 @@
 CAP = 4
 OFFSETS = (-2, -1, 1, 2)
 SENT_FIRST = (0, 3, 1, 2)
-PIECES = 2
+PIECES = 1
 PIECE = CAP // PIECES
 MESH = pl.DeviceIdType.MESH
 
@@ -339,31 +339,33 @@
                 adv[s, c, 1 + r * 8 + i] = done[i]
             return 0
 
-        several(np_, 4, own, 0)
+        several(np_, 8, own, 0)
         odd = lax.rem(lat, 2)
 
-        def arrivals(t, _):
-            turn, h = t // PIECES, lax.rem(t, PIECES)
-            o = jnp.where(turn == 0, 2 - odd, jnp.where(turn == 3, 1 + odd, 3 * (turn - 1)))
+        def come(o, j):
+            e = ti[(s * 4 + o) * CAP + j, 1]
+            block = arr[s, o, j]
+            done = interpolate([block[i] for i in range(8)], weights(s, e), ratio)
+            for i in range(8):
+                ia[s, o * CAP + j, i] = done[i]
+
+        def arrived(o):
             offset = o - 2 + jnp.where(o >= 2, 1, 0)
 
             @pl.when(in_range(offset))
             def _():
-                piece = arr.at[s, o, pl.ds(h * PIECE, PIECE)]
-                pltpu.make_async_copy(piece, piece, precv.at[s, o, h]).wait()
-                for k in range(PIECE):
-                    j = h * PIECE + k
-                    e = ti[(s * 4 + o) * CAP + j, 1]
-                    block = arr[s, o, j]
-                    done = interpolate(
-                        [block[i] for i in range(8)], weights(s, e), ratio
-                    )
-                    for i in range(8):
-                        ia[s, o * CAP + j, i] = done[i]
-
-            return 0
-
-        lax.fori_loop(0, 4 * PIECES, arrivals, 0)
+                piece = arr.at[s, o]
+                pltpu.make_async_copy(piece, piece, precv.at[s, o, 0]).wait()
+
+        arrived(2 - odd)
+        for j in range(CAP):
+            come(2 - odd, j)
+        far = (0, 3, 1 + odd)
+        for o in far:
+            arrived(o)
+        for o in far:
+            for j in range(CAP):
+                come(o, j)
 
         def join(q, total):
             c, r = q // br, lax.rem(q, br)
@@ -377,7 +379,7 @@
                 total = total + weight[r * 8 + i] * v
             return total
 
-        total = several(np_, 4, join, zero)
+        total = several(np_, 8, join, zero)
         for i in range(2):
 
             @pl.when(in_range(2 * i - 1))
@@ -492,7 +494,7 @@
             st[in_state(row, c)] = done[c]
         return 0
 
-    several(rows, 4, first_step, 0)
+    several(rows, 8, first_step, 0)
     wait_halos(0)
     add_halos(0, (st, in_state))
     send_patches(1, [ti[4 * CAP + k, 0] for k in range(4 * CAP)])
@@ -514,7 +516,7 @@
             out[in_out(row, c)] = done[c]
         return 0
 
-    several(rows, 4, last_step, 0)
+    several(rows, 8, last_step, 0)
     wait_halos(1)
     add_halos(1, (out, in_out))
     ratio = jnp.broadcast_to(target / masses_sum(1)[0:1], (8, values))
@@ -524,7 +526,7 @@
             out[in_out(row, c)] = out[in_out(row, c)] * ratio
         return 0
 
-    several(rows, 4, scale, 0)
+    several(rows, 8, scale, 0)
 
     for s in range(STEPS):
         for o in range(4):

time: 31 us -> 30.3 us (0.977)
  Pallas kernels: 29.9 us -> 29.2 us
    pallas_call x1, Pallas kernels: 29.9 us -> 29.2 us  [local(): pl.pallas_call(functools.partial(kernel, br, bc, lats, lons), out_shape=p...]
where the time goes in v5:
time: 30.3 us; the launch traced here: 30.2 us
  Pallas kernels  29.2 us (96%)
  local copies, waits for them, and re-layouts  0.97 us (3%)
    pallas_call x1, Pallas kernels, local(): pl.pallas_call(functools.partial(kernel, br, bc, lats, lons), out_shape=p...  29.2 us
    unnamed x1, local copies, waits for them, and re-layouts  0.97 us

profile of v5, /device:TPU:0, one launch (start us, length us, event | category | flops | bytes accessed | tf_op | source)
XLA Modules:
  0.0 30.2 jit_solution(13767365573421729370)
XLA Ops:
  0.0 29.2 %shard_map.46 = f32[4,8,8,8,128]{4,3,2,1,0:T(8,128)S(1)} custom-call(s32[2,16,32]{2,1,0:T(8,128)} %source_hbm.1, f32[2,3,16,32]{3,2,1,0:T(8,128)} %shift_hbm.1, f32[32]{0:T(128)} %kappa_hbm.1, f32[4,8,8,8,128]{4,3,2,1,0:T(8,128)} %bitcast.3), custom_call_target="tpu_custom_call" | custom-call | tf_op jit(solution)/shard_map/pallas_call | solution.py:563
  29.2 1.0 %copy.6 = f32[32,64,128]{2,1,0:T(8,128)} copy(f32[32,64,128]{2,1,0:T(8,128)S(1)} %bitcast.2) | data formatting | bytes 2097152

commit v6 on v5

--- a/solution.py
+++ b/solution.py
@@ -41,7 +41,7 @@
     values = rows[0].shape[1]
     step = values // LEV
     column = lax.broadcasted_iota(jnp.int32, (8, values), 0)
-    level = lax.broadcasted_iota(jnp.int32, (8, values), 1) // step
+    level = quotient(lax.broadcasted_iota(jnp.int32, (8, values), 1), step)
     wy, wx, wz = (
         [jnp.full((8, values), w, jnp.float32) for w in part] for part in weights
     )
@@ -91,7 +91,7 @@
     sub = lax.broadcasted_iota(jnp.int32, (8, lanes), 0)
     at = lax.broadcasted_iota(jnp.int32, (total_cols, lanes), 0)
     entry = lax.broadcasted_iota(jnp.int32, (total_cols, lanes), 1)
-    pick_columns = jnp.where(at == lon * bc + entry % bc, 1.0, 0.0)
+    pick_columns = jnp.where(at == lon * bc + entry - quotient(entry, bc) * bc, 1.0, 0.0)
     near[...] = jnp.dot(
         source[...].reshape(STEPS * lat_rows, total_cols).astype(jnp.float32),
         pick_columns,
@@ -104,7 +104,7 @@
         precision=lax.Precision.HIGHEST,
         preferred_element_type=jnp.float32,
     )
-    row_of = lax.broadcasted_iota(jnp.int32, (br, lanes), 1) // bc
+    row_of = quotient(lax.broadcasted_iota(jnp.int32, (br, lanes), 1), bc)
     own_row = row_of == lax.broadcasted_iota(jnp.int32, (br, lanes), 0)
 
     def band(ref, first):
@@ -156,9 +156,9 @@
 
         outer = (0, 1, 3, 4)
         slot = lax.broadcasted_iota(jnp.int32, (4 * CAP, lanes), 0)
-        which = slot // CAP
+        which = quotient(slot, CAP)
+        slot = slot - which * CAP
         which = jnp.where(which >= 2, which + 1, which)
-        slot = slot % CAP
         place = lax.broadcasted_iota(jnp.int32, (4 * CAP, lanes), 1)
         sent = jnp.where(spread(code, outer) == slot, spread(source_q, outer), 0)
         mine = (2,) * 4
@@ -181,13 +181,12 @@
     return first_sent
 
 
-def several(count, unroll, body, carry):
-    def turn(i, carry):
-        for k in range(unroll):
-            carry = body(i * unroll + k, carry)
-        return carry
-
-    return lax.fori_loop(0, count // unroll, turn, carry)
+def each_band(br, body, carry):
+    return lax.fori_loop(0, br, body, carry)
+
+
+def wrapped(x, n):
+    return jnp.where(x >= n, x - n, x)
 
 
 def kernel(
@@ -229,18 +228,12 @@
     row_in[...] = jnp.zeros_like(row_in)
 
     def peer(k):
-        return {
-            "lat": lax.rem(lat + k // lons, lats),
-            "lon": lax.rem(lon + lax.rem(k, lons), lons),
-        }
+        return {"lat": wrapped(lat + k // lons, lats), "lon": wrapped(lon + k % lons, lons)}
 
     barrier = pltpu.get_barrier_semaphore()
 
-    def greet(k, _):
+    for k in range(1, peers):
         pl.semaphore_signal(barrier, inc=1, device_id=peer(k), device_id_type=MESH)
-        return 0
-
-    lax.fori_loop(1, peers, greet, 0)
     for copy in small:
         copy.wait()
     first_sent = make_tables(
@@ -293,7 +286,7 @@
             dst_ref=side_in.at[s, 1 - i],
             send_sem=hsend.at[s, 2 + i],
             recv_sem=hrecv.at[s, 3 - i],
-            device_id={"lat": lat, "lon": lax.rem(lon + lons + 2 * i - 1, lons)},
+            device_id={"lat": lat, "lon": wrapped(lon + (1 if i else lons - 1), lons)},
             device_id_type=MESH,
         )
 
@@ -311,7 +304,7 @@
         return [[tf[8 * k + s * 3 + i, e] for k in range(4)] for i in range(3)]
 
     def masses(s):
-        def send(k, _):
+        for k in range(1, peers):
             pltpu.make_async_remote_copy(
                 src_ref=mass_out.at[s],
                 dst_ref=mass_in.at[s, k],
@@ -320,9 +313,6 @@
                 device_id=peer(k),
                 device_id_type=MESH,
             ).start()
-            return 0
-
-        lax.fori_loop(1, peers, send, 0)
 
     def masses_sum(s):
         others = mass_in.at[s, pl.ds(1, peers - 1)]
@@ -330,17 +320,17 @@
         return jnp.sum(mass_in[s], axis=0)
 
     def advect(s, ratio):
-        def own(q, _):
-            c, r = q // br, lax.rem(q, br)
-            e = r * bc + c
-            block = st[s, ti[STEPS * 4 * CAP + 2 * s, e]]
-            done = interpolate([block[i] for i in range(8)], weights(s, e), ratio)
-            for i in range(8):
-                adv[s, c, 1 + r * 8 + i] = done[i]
+        def own(r, _):
+            for c in range(bc):
+                e = r * bc + c
+                block = st[s, ti[STEPS * 4 * CAP + 2 * s, e]]
+                done = interpolate([block[i] for i in range(8)], weights(s, e), ratio)
+                for i in range(8):
+                    adv[s, c, 1 + r * 8 + i] = done[i]
             return 0
 
-        several(np_, 8, own, 0)
-        odd = lax.rem(lat, 2)
+        each_band(br, own, 0)
+        odd = lat & 1
 
         def come(o, j):
             e = ti[(s * 4 + o) * CAP + j, 1]
@@ -367,19 +357,21 @@
             for j in range(CAP):
                 come(o, j)
 
-        def join(q, total):
-            c, r = q // br, lax.rem(q, br)
-            e = r * bc + c
-            pick = ti[STEPS * 4 * CAP + 2 * s + 1, e]
-            block = ia[s, jnp.maximum(pick, 0)]
-            far = jnp.full((8, values), pick, jnp.int32) >= 0
+        def join(r, total):
+            sums = [zero] * 8
+            for c in range(bc):
+                pick = ti[STEPS * 4 * CAP + 2 * s + 1, r * bc + c]
+                block = ia[s, jnp.maximum(pick, 0)]
+                far = jnp.full((8, values), pick, jnp.int32) >= 0
+                for i in range(8):
+                    v = jnp.where(far, block[i], adv[s, c, 1 + r * 8 + i])
+                    adv[s, c, 1 + r * 8 + i] = v
+                    sums[i] = sums[i] + v
             for i in range(8):
-                v = jnp.where(far, block[i], adv[s, c, 1 + r * 8 + i])
-                adv[s, c, 1 + r * 8 + i] = v
-                total = total + weight[r * 8 + i] * v
+                total = total + weight[r * 8 + i] * sums[i]
             return total
 
-        total = several(np_, 8, join, zero)
+        total = each_band(br, join, zero)
         for i in range(2):
 
             @pl.when(in_range(2 * i - 1))
@@ -410,18 +402,20 @@
         ref, where = place
         for i, row in enumerate((0, rows - 1)):
             for c in range(bc):
-                at = where(row, c)
+                at = where(row // 8, row % 8, c)
                 ref[at] = ref[at] + kappa[row] * row_in[s, i, c]
 
-        def sides(row, _):
-            for i, c in enumerate((0, bc - 1)):
-                at = where(row, c)
-                side = jnp.broadcast_to(side_in[s, i, pl.ds(row, 1)], (8, values))
-                side = jnp.where(column == (7 if i else 0), side, 0.0)
-                ref[at] = ref[at] + kappa[row] * side
+        def sides(r, _):
+            for a in range(8):
+                row = r * 8 + a
+                for i, c in enumerate((0, bc - 1)):
+                    at = where(r, a, c)
+                    side = jnp.broadcast_to(side_in[s, i, pl.ds(row, 1)], (8, values))
+                    side = jnp.where(column == (7 if i else 0), side, 0.0)
+                    ref[at] = ref[at] + kappa[row] * side
             return 0
 
-        several(rows, 8, sides, 0)
+        each_band(br, sides, 0)
 
     def diffused_row(s, row):
         here = [adv[s, c, 1 + row] for c in range(bc)]
@@ -462,11 +456,13 @@
             w = w + area(row + 1) * kappa[row + 1]
         weight[row] = w
 
-    def target_row(row, total):
-        parts = [st[0, c * br + row // 8, lax.rem(row, 8)] for c in range(bc)]
-        return total + area(row) * functools.reduce(jnp.add, parts)
-
-    target_part = several(rows, 4, target_row, zero)
+    def target_band(r, total):
+        for a in range(8):
+            parts = [st[0, c * br + r, a] for c in range(bc)]
+            total = total + area(r * 8 + a) * functools.reduce(jnp.add, parts)
+        return total
+
+    target_part = each_band(br, target_band, zero)
     for i in range(2):
 
         @pl.when(in_range(2 * i - 1))
@@ -485,16 +481,17 @@
     mass_in[0, 0] = both
     masses(0)
 
-    def in_state(row, c):
-        return 1, c * br + row // 8, row % 8 if isinstance(row, int) else lax.rem(row, 8)
-
-    def first_step(row, _):
-        done = diffused_row(0, row)
-        for c in range(bc):
-            st[in_state(row, c)] = done[c]
+    def in_state(r, a, c):
+        return 1, c * br + r, a
+
+    def first_step(r, _):
+        for a in range(8):
+            done = diffused_row(0, r * 8 + a)
+            for c in range(bc):
+                st[in_state(r, a, c)] = done[c]
         return 0
 
-    several(rows, 8, first_step, 0)
+    each_band(br, first_step, 0)
     wait_halos(0)
     add_halos(0, (st, in_state))
     send_patches(1, [ti[4 * CAP + k, 0] for k in range(4 * CAP)])
@@ -507,26 +504,28 @@
     mass_in[1, 0] = both
     masses(1)
 
-    def in_out(row, c):
-        return row // 8, row % 8 if isinstance(row, int) else lax.rem(row, 8), c
-
-    def last_step(row, _):
-        done = diffused_row(1, row)
-        for c in range(bc):
-            out[in_out(row, c)] = done[c]
+    def in_out(r, a, c):
+        return r, a, c
+
+    def last_step(r, _):
+        for a in range(8):
+            done = diffused_row(1, r * 8 + a)
+            for c in range(bc):
+                out[in_out(r, a, c)] = done[c]
         return 0
 
-    several(rows, 8, last_step, 0)
+    each_band(br, last_step, 0)
     wait_halos(1)
     add_halos(1, (out, in_out))
     ratio = jnp.broadcast_to(target / masses_sum(1)[0:1], (8, values))
 
-    def scale(row, _):
-        for c in range(bc):
-            out[in_out(row, c)] = out[in_out(row, c)] * ratio
+    def scale(r, _):
+        for a in range(8):
+            for c in range(bc):
+                out[r, a, c] = out[r, a, c] * ratio
         return 0
 
-    several(rows, 8, scale, 0)
+    each_band(br, scale, 0)
 
     for s in range(STEPS):
         for o in range(4):

time: 30.3 us -> 29.3 us (0.967)
  Pallas kernels: 29.2 us -> 28.1 us
    pallas_call x1, Pallas kernels: 29.2 us -> 28.1 us  [local(): pl.pallas_call(functools.partial(kernel, br, bc, lats, lons), out_shape=p...]
where the time goes in v6:
time: 29.3 us; the launch traced here: 29.1 us
  Pallas kernels  28.1 us (96%)
  local copies, waits for them, and re-layouts  0.97 us (3%)
    pallas_call x1, Pallas kernels, local(): pl.pallas_call(functools.partial(kernel, br, bc, lats, lons), out_shape=p...  28.1 us
    unnamed x1, local copies, waits for them, and re-layouts  0.97 us

profile of v6, /device:TPU:0, one launch (start us, length us, event | category | flops | bytes accessed | tf_op | source)
XLA Modules:
  0.0 29.1 jit_solution(10326614142470645666)
XLA Ops:
  0.0 28.1 %shard_map.46 = f32[4,8,8,8,128]{4,3,2,1,0:T(8,128)S(1)} custom-call(s32[2,16,32]{2,1,0:T(8,128)} %source_hbm.1, f32[2,3,16,32]{3,2,1,0:T(8,128)} %shift_hbm.1, f32[32]{0:T(128)} %kappa_hbm.1, f32[4,8,8,8,128]{4,3,2,1,0:T(8,128)} %bitcast.3), custom_call_target="tpu_custom_call" | custom-call | tf_op jit(solution)/shard_map/pallas_call | solution.py:562
  28.2 1.0 %copy.6 = f32[32,64,128]{2,1,0:T(8,128)} copy(f32[32,64,128]{2,1,0:T(8,128)S(1)} %bitcast.2) | data formatting | bytes 2097152

commit v7 on v6

--- a/solution.py
+++ b/solution.py
@@ -13,7 +13,7 @@
 CAP = 4
 OFFSETS = (-2, -1, 1, 2)
 SENT_FIRST = (0, 3, 1, 2)
-PIECES = 1
+PIECES = 2
 PIECE = CAP // PIECES
 MESH = pl.DeviceIdType.MESH
 
@@ -339,23 +339,25 @@
             for i in range(8):
                 ia[s, o * CAP + j, i] = done[i]
 
-        def arrived(o):
+        def arrived(o, halves):
             offset = o - 2 + jnp.where(o >= 2, 1, 0)
 
             @pl.when(in_range(offset))
             def _():
-                piece = arr.at[s, o]
-                pltpu.make_async_copy(piece, piece, precv.at[s, o, 0]).wait()
-
-        arrived(2 - odd)
-        for j in range(CAP):
-            come(2 - odd, j)
-        far = (0, 3, 1 + odd)
-        for o in far:
-            arrived(o)
-        for o in far:
-            for j in range(CAP):
-                come(o, j)
+                for h in range(PIECES):
+                    piece = arr.at[s, o, pl.ds(h * PIECE, PIECE)]
+                    pltpu.make_async_copy(piece, piece, precv.at[s, o, h]).wait()
+                    if halves:
+                        for j in range(h * PIECE, (h + 1) * PIECE):
+                            come(o, j)
+                if not halves:
+                    for j in range(CAP):
+                        come(o, j)
+
+        arrived(2 - odd, False)
+        arrived(0, False)
+        arrived(3, False)
+        arrived(1 + odd, True)
 
         def join(r, total):
             sums = [zero] * 8

time: 29.3 us -> 29.2 us (level)
  no operation moved by 1% of the time
where the time goes in v7:
time: 29.2 us; the launch traced here: 29.1 us
  Pallas kernels  28.1 us (96%)
  local copies, waits for them, and re-layouts  0.97 us (3%)
    pallas_call x1, Pallas kernels, local(): pl.pallas_call(functools.partial(kernel, br, bc, lats, lons), out_shape=p...  28.1 us
    unnamed x1, local copies, waits for them, and re-layouts  0.97 us

profile of v7, /device:TPU:0, one launch (start us, length us, event | category | flops | bytes accessed | tf_op | source)
XLA Modules:
  0.0 29.1 jit_solution(147347972877345498)
XLA Ops:
  0.0 28.1 %shard_map.46 = f32[4,8,8,8,128]{4,3,2,1,0:T(8,128)S(1)} custom-call(s32[2,16,32]{2,1,0:T(8,128)} %source_hbm.1, f32[2,3,16,32]{3,2,1,0:T(8,128)} %shift_hbm.1, f32[32]{0:T(128)} %kappa_hbm.1, f32[4,8,8,8,128]{4,3,2,1,0:T(8,128)} %bitcast.3), custom_call_target="tpu_custom_call" | custom-call | tf_op jit(solution)/shard_map/pallas_call | solution.py:564
  28.1 1.0 %copy.6 = f32[32,64,128]{2,1,0:T(8,128)} copy(f32[32,64,128]{2,1,0:T(8,128)S(1)} %bitcast.2) | data formatting | bytes 2097152

commit v8 on v7

--- a/solution.py
+++ b/solution.py
@@ -191,7 +191,7 @@
 
 def kernel(
     br, bc, lats, lons,
-    source_hbm, shift_hbm, kappa_hbm, tr, out,
+    source_hbm, shift_hbm, kappa_hbm, tr, out, ratio_out,
     st, arr, ia, snd, adv, row_in, side_out, side_in, ka_out, ka_in, mass_out, mass_in,
     source, shift, near, near_shift, ti_v, tf_v, ti, tf, kappa, weight,
     load_sem, small_sem, psend, precv, hsend, hrecv, ksend, krecv, msend, mrecv,
@@ -519,15 +519,7 @@
     each_band(br, last_step, 0)
     wait_halos(1)
     add_halos(1, (out, in_out))
-    ratio = jnp.broadcast_to(target / masses_sum(1)[0:1], (8, values))
-
-    def scale(r, _):
-        for a in range(8):
-            for c in range(bc):
-                out[r, a, c] = out[r, a, c] * ratio
-        return 0
-
-    each_band(br, scale, 0)
+    ratio_out[...] = jnp.broadcast_to(target / masses_sum(1)[0:1], (8, values))
 
     for s in range(STEPS):
         for o in range(4):
@@ -551,6 +543,25 @@
         @pl.when(in_range(2 * i - 1))
         def _():
             ka_copy(i).wait_send()
+
+
+def scale_kernel(field, ratio, out, scaled, sems):
+    br, _, bc = field.shape[:3]
+    factor = ratio[...]
+    copies = []
+    for r in range(br):
+        for h in range(2):
+            for a in range(4 * h, 4 * h + 4):
+                for c in range(bc):
+                    scaled[r, a, c] = field[r, a, c] * factor
+            part = pl.ds(4 * h, 4)
+            copy = pltpu.make_async_copy(
+                scaled.at[r, part], out.at[r, part], sems.at[r, h]
+            )
+            copy.start()
+            copies.append(copy)
+    for copy in copies:
+        copy.wait()
 
 
 def local(lats, lons, tracers, shifts, diffusivity, source_patch):
@@ -561,16 +572,16 @@
     peers = lats * lons
     dma = pltpu.SemaphoreType.DMA
     f32 = jnp.float32
-    result = pl.pallas_call(
+    field, ratio = pl.pallas_call(
         functools.partial(kernel, br, bc, lats, lons),
-        out_shape=pltpu.VMEM((br, 8, bc, 8, values), f32),
+        out_shape=(pltpu.VMEM((br, 8, bc, 8, values), f32), pltpu.VMEM((8, values), f32)),
         in_specs=[
             pl.BlockSpec(memory_space=pltpu.HBM),
             pl.BlockSpec(memory_space=pltpu.HBM),
             pl.BlockSpec(memory_space=pltpu.HBM),
             pl.BlockSpec(memory_space=pltpu.HBM),
         ],
-        out_specs=pl.BlockSpec(memory_space=pltpu.VMEM),
+        out_specs=(pl.BlockSpec(memory_space=pltpu.VMEM),) * 2,
         scratch_shapes=[
             pltpu.VMEM((STEPS, np_) + tile, f32),
             pltpu.VMEM((STEPS, 4, CAP) + tile, f32),
@@ -619,6 +630,13 @@
             )
         )
     )
+    result = pl.pallas_call(
+        scale_kernel,
+        out_shape=jax.ShapeDtypeStruct(field.shape, f32),
+        in_specs=[pl.BlockSpec(memory_space=pltpu.VMEM)] * 2,
+        out_specs=pl.BlockSpec(memory_space=pltpu.HBM),
+        scratch_shapes=[pltpu.VMEM(field.shape, f32), dma((br, 2))],
+    )(field, ratio)
     return result.reshape(rows, cols, values)
 
 

time: 29.2 us -> 32 us (1.096)
  Pallas kernels: 28.1 us -> 30.3 us
  local copies, waits for them, and re-layouts: 0.97 us -> 1.56 us
    pallas_call x1 -> x2, Pallas kernels: 28.1 us -> 30.3 us  [the longest x1 28 us: local(): pl.pallas_call(functools.partial(kernel, br, bc, lats, lons), out_shape=(...]
    unnamed x1 -> x4, local copies, waits for them, and re-layouts: 0.97 us -> 1.56 us
where the time goes in v8:
time: 32 us; the launch traced here: 31.8 us
  Pallas kernels  30.3 us (95%)
  local copies, waits for them, and re-layouts  1.56 us (5%)
    pallas_call x1, Pallas kernels, local(): pl.pallas_call(functools.partial(kernel, br, bc, lats, lons), out_shape=(...  28 us
    pallas_call x1, Pallas kernels, local(): pl.pallas_call(scale_kernel, out_shape=jax.ShapeDtypeStruct(field.shape,...  2.26 us
    unnamed x4, local copies, waits for them, and re-layouts  1.56 us

profile of v8, /device:TPU:0, one launch (start us, length us, event | category | flops | bytes accessed | tf_op | source)
XLA Modules:
  0.0 31.8 jit_solution(12778810099764760100)
XLA Ops:
  0.0 28.0 %shard_map.46 = (f32[4,8,8,8,128]{4,3,2,1,0:T(8,128)S(1)}, f32[8,128]{1,0:T(8,128)S(1)}) custom-call(s32[2,16,32]{2,1,0:T(8,128)} %source_hbm.1, f32[2,3,16,32]{3,2,1,0:T(8,128)} %shift_hbm.1, f32[32]{0:T(128)} %kappa_hbm.1, f32[4,8,8,8,128]{4,3,2,1,0:T(8,128)} %bitcast.2), custom_call_target="tpu_custom_call" | custom-call | tf_op jit(solution)/shard_map/pallas_call | solution.py:575
  28.0 0.0 copy-start
  28.0 1.0 %copy-done = f32[4,8,8,8,128]{4,3,2,1,0:T(8,128)} copy-done((f32[4,8,8,8,128]{4,3,2,1,0:T(8,128)}, f32[4,8,8,8,128]{4,3,2,1,0:T(8,128)S(1)}, u32[]{:S(2)}) %copy-start) | copy-done | bytes 1048600
  29.0 0.0 copy-start.1
  29.0 0.6 %copy-done.1 = f32[8,128]{1,0:T(8,128)} copy-done((f32[8,128]{1,0:T(8,128)}, f32[8,128]{1,0:T(8,128)S(1)}, u32[]{:S(2)}) %copy-start.1) | copy-done | bytes 4120
  29.6 2.3 %shard_map.47 = f32[4,8,8,8,128]{4,3,2,1,0:T(8,128)} custom-call(f32[4,8,8,8,128]{4,3,2,1,0:T(8,128)} %copy-done, f32[8,128]{1,0:T(8,128)} %copy-done.1), custom_call_target="tpu_custom_call" | custom-call | tf_op jit(solution)/shard_map/pallas_call | solution.py:633
Async XLA Ops:
  28.0 1.0 %copy-start = (f32[4,8,8,8,128]{4,3,2,1,0:T(8,128)}, f32[4,8,8,8,128]{4,3,2,1,0:T(8,128)S(1)}, u32[]{:S(2)}) copy-start(f32[4,8,8,8,128]{4,3,2,1,0:T(8,128)S(1)} %get-tuple-element.7.field) | copy-start | bytes 3145732
  29.0 0.6 %copy-start.1 = (f32[8,128]{1,0:T(8,128)}, f32[8,128]{1,0:T(8,128)S(1)}, u32[]{:S(2)}) copy-start(f32[8,128]{1,0:T(8,128)S(1)} %get-tuple-element.8.ratio) | copy-start | bytes 12292
